TPU v7x, 1024 devices: a whole 4x8x16 slice. The times are simulated.
1024 devices in a mesh: group: 32 (over z, core), member: 32 (over y, x).
Axes of the slice: x: 4, y: 8, z: 16, core: 2. Of those that a mesh axis runs over, the one named last changes fastest.
Arguments:
- source: float32 [1024, 1024, 128], P('group', 'member'), may hold values from -5 to 8
- potential: float32 [1024, 1024, 128], P('group', 'member'), may hold values from -3 to 3
- refined: int32 [32, 32, 4], P('group', 'member'), may hold values 0 or 1
Outputs:
- smoothed: float32 [1024, 1024, 128], P('group', 'member')
- residual: float32 [1024, 1024, 128], P('group', 'member')
Inputs may be any that keep to these rules, and one draw needn't show every extreme that they name: 1 marks a refined box, 0 one that is not smoothed on the fine level.
All inputs are finite; a program needn't handle non-finite values. No bound on the sum of `refined` on one device may be relied on, other than what follows from the above.
Results may differ from a plain program's by a relative error of at most 0.000035.
Values sent between devices are 32-bit elements; how exact they have to be, the bound alone decides.
No kernel may reach another device: no remote copies, remote signals or barrier semaphores. Data moves between devices by JAX's collectives and lax.ppermute only.
A program may use at most 128 MiB of HBM per device.

v0:
```python
import functools

import jax
import jax.numpy as jnp
from jax import lax
from jax.sharding import Mesh
from jax.sharding import PartitionSpec as P

PRE = 2
POST = 2
COARSE = 2
GROUP_MEMBER = ("group_0", "group_1", "member_0", "member_1")
GROUP = ("group_0", "group_1")
MEMBER = ("member_0", "member_1")


def extended(shard, sides, width):
    edges = {}
    for axis, dim in sides:
        size, length = (lax.axis_size(axis), shard.shape[dim])
        up = [(i, (i + 1) % size) for i in range(size - 1)]
        last = lax.slice_in_dim(shard, length - width, length, axis=dim)
        initial = lax.slice_in_dim(shard, 0, width, axis=dim)
        edges[dim] = (
            lax.ppermute(last, axis, up),
            lax.ppermute(initial, axis, [(b, a) for a, b in up]),
        )
    done = []
    for _, dim in sides:
        low, high = edges[dim]
        around = [(width, width) if d in done else (0, 0) for d in range(shard.ndim)]
        shard = jnp.concatenate([jnp.pad(low, around), shard, jnp.pad(high, around)], axis=dim)
        done.append(dim)
    return shard


def with_halo(cells, sides, width):
    for axis, dim in sides:
        count = lax.axis_size(axis)
        ends = count - 1
        head = lax.slice_in_dim(cells, 0, width, axis=dim)
        tail = lax.slice_in_dim(cells, cells.shape[dim] - width, cells.shape[dim], axis=dim)
        cells = jnp.concatenate(
            [
                lax.ppermute(tail, axis, [(i, (i + 1) % count) for i in range(ends)]),
                cells,
                lax.ppermute(head, axis, [((i + 1) % count, i) for i in range(ends)]),
            ],
            axis=dim,
        )
    return cells


def by_axis(shard, axes):
    return functools.reduce(lax.psum, axes, shard)


def stencil_sum(padded):
    total = padded[2:, 1:-1, 1:-1] + padded[:-2, 1:-1, 1:-1]
    total = total + padded[1:-1, 2:, 1:-1] + padded[1:-1, :-2, 1:-1]
    return total + padded[1:-1, 1:-1, 2:] + padded[1:-1, 1:-1, :-2]


def expand(values_in, factor):
    size_a, size_b, size_c = values_in.shape
    wide = jnp.broadcast_to(
        values_in[:, None, :, None, :, None], (size_a, factor, size_b, factor, size_c, factor)
    )
    return wide.reshape(size_a * factor, size_b * factor, size_c * factor)


def parity_at(shape, offset_x, offset_y):
    along_x = lax.broadcasted_iota(jnp.int32, shape, 0) + offset_x
    along_y = lax.broadcasted_iota(jnp.int32, shape, 1) + offset_y
    along_z = lax.broadcasted_iota(jnp.int32, shape, 2)
    return (along_x + along_y + along_z) % 2


def fine_padded(grid_field):
    padded = extended(grid_field, ((GROUP, 0), (MEMBER, 1)), 1)
    return jnp.pad(padded, ((0, 0), (0, 0), (1, 1)))


def slab_padded(grid_field):
    padded = with_halo(grid_field, ((GROUP, 0),), 1)
    return jnp.pad(padded, ((0, 0), (1, 1), (1, 1)))


def red_black(grid_field, right_side, active, parity, padder):
    for colour in (0, 1):
        update = (right_side + stencil_sum(padder(grid_field))) / 6.0
        grid_field = jnp.where((parity == colour) & active, update, grid_field)
    return grid_field


def wide_sweeps(grid_field, right_side, active_flags, offset_x, offset_y, count):
    depth = 2 * count
    stacked = jnp.stack([grid_field, right_side, active_flags])
    wide = with_halo(stacked, ((GROUP, 1), (MEMBER, 2)), depth)
    field_wide = wide[0]
    right_wide = wide[1]
    mask_wide = wide[2] > 0.5
    parity_wide = parity_at(field_wide.shape, offset_x - depth, offset_y - depth)
    for _ in range(count):
        for colour in (0, 1):
            update = (right_wide + stencil_sum(jnp.pad(field_wide, 1))) / 6.0
            field_wide = jnp.where((parity_wide == colour) & mask_wide, update, field_wide)
    return field_wide[depth:-depth, depth:-depth, :]


def per_device(source, potential, refined):
    cells_x, cells_y, cells_z = source.shape
    groups = lax.axis_size(GROUP)
    members = lax.axis_size(MEMBER)
    group_at = lax.axis_index(GROUP)
    member_at = lax.axis_index(MEMBER)
    total_cells = cells_x * cells_y * cells_z * groups * members
    density_mean = by_axis(jnp.sum(source), GROUP_MEMBER) / total_cells
    contrast = source - density_mean
    active = expand(refined == 1, cells_x)
    active_flags = active.astype(jnp.float32)
    phi = potential
    phi = wide_sweeps(phi, contrast, active_flags, group_at * cells_x, member_at * cells_y, PRE)
    fine_residual = contrast - (6.0 * phi - stencil_sum(fine_padded(phi)))
    half_x, half_y, half_z = (cells_x // 2, cells_y // 2, cells_z // 2)
    coarse_source = fine_residual.reshape(half_x, 2, half_y, 2, half_z, 2).sum(axis=(1, 3, 5)) * 0.5
    reach = 2 * COARSE
    widened = with_halo(coarse_source, ((MEMBER, 1),), reach)
    slab_parity = parity_at(widened.shape, group_at * half_x, member_at * half_y - reach)
    global_y = lax.broadcasted_iota(jnp.int32, widened.shape, 1) + member_at * half_y - reach
    inside = (global_y >= 0) & (global_y < half_y * members)
    correction = jnp.zeros(widened.shape, jnp.float32)
    for _ in range(COARSE):
        correction = red_black(correction, widened, inside, slab_parity, slab_padded)
    correction = correction[:, reach : reach + half_y, :]
    phi = phi + expand(correction, 2)
    phi = wide_sweeps(phi, contrast, active_flags, group_at * cells_x, member_at * cells_y, POST)
    residual = contrast - (6.0 * phi - stencil_sum(fine_padded(phi)))
    return (phi, residual)


def solution(mesh):
    finer = Mesh(mesh.devices.reshape(16, 2, 8, 4), ("group_0", "group_1", "member_0", "member_1"))
    return jax.shard_map(
        per_device,
        mesh=finer,
        in_specs=(P(GROUP, MEMBER, None), P(GROUP, MEMBER, None), P(GROUP, MEMBER, None)),
        out_specs=(P(GROUP, MEMBER, None), P(GROUP, MEMBER, None)),
        check_vma=False,
    )
```

profile of v0, /device:TPU:223, one launch (start us, length us, event | category | flops | bytes accessed | tf_op | source)
XLA Modules:
  0.0 290.4 jit_solution(540669601768003397)
XLA Ops:
  0.6 1.8 reduce_sum.18
  2.5 30.3 %psum.28 = f32[]{:T(128)} all-reduce(f32[]{:T(128)} %reduce_sum.18), channel_id=1, replica_groups=mesh['group_0'=16,'group_1'=2,'member_0'=8,'member_1'=4] {'group_0'}, use_global_device_ids=true, to_apply=%region_1.0 | all-reduce | flops 1 | bytes 8 | tf_op jit(solution)/shard_map/psum | solution.py:55
  32.8 10.1 %psum.29 = f32[]{:T(128)} all-reduce(f32[]{:T(128)} %psum.28), channel_id=1, replica_groups=mesh['group_0'=16,'group_1'=2,'member_0'=8,'member_1'=4] {'group_1'}, use_global_device_ids=true, to_apply=%region_2.0 | all-reduce | flops 1 | bytes 8 | tf_op jit(solution)/shard_map/psum | solution.py:55
  42.9 12.9 %psum.30 = f32[]{:T(128)} all-reduce(f32[]{:T(128)} %psum.29), channel_id=1, replica_groups=mesh['group_0'=16,'group_1'=2,'member_0'=8,'member_1'=4] {'member_0'}, use_global_device_ids=true, to_apply=%region_3.0 | all-reduce | flops 1 | bytes 8 | tf_op jit(solution)/shard_map/psum | solution.py:55
  55.7 6.4 %psum.31 = f32[]{:T(128)} all-reduce(f32[]{:T(128)} %psum.30), channel_id=1, replica_groups=mesh['group_0'=16,'group_1'=2,'member_0'=8,'member_1'=4] {'member_1'}, use_global_device_ids=true, to_apply=%region_4.0 | all-reduce | flops 1 | bytes 8 | tf_op jit(solution)/shard_map/psum | solution.py:55
  62.8 1.1 subtract_bitcast_fusion
  63.8 0.7 fusion.118
  64.9 9.7 %collective-permute-start = (f32[3,4,32,128]{3,2,1,0:T(8,128)S(1)}, f32[3,4,32,128]{3,2,1,0:T(8,128)S(1)}, u32[]{:S(2)}, u32[]{:S(2)}) collective-permute-start(f32[3,4,32,128]{3,2,1,0:T(8,128)S(1)} %get-tuple-element.12), channel_id=1, source_target_pairs={{0,32},{32,64},{64,96},{96,128},{128,160},{160,192},{192,224},{224... | collective-permute-start | bytes 589832 | tf_op jit(solution)/shard_map/ppermute | solution.py:45
  74.6 1.9 collective-permute-start.1
  76.6 1.9 collective-permute-start.10
  78.5 4.3 %collective-permute-done.1 = f32[3,4,32,128]{3,2,1,0:T(8,128)S(1)} collective-permute-done((f32[3,4,32,128]{3,2,1,0:T(8,128)S(1)}, f32[3,4,32,128]{3,2,1,0:T(8,128)S(1)}, u32[]{:S(2)}, u32[]{:S(2)}) %collective-permute-start.1) | collective-permute-done | bytes 196640 | tf_op jit(solution)/shard_map/ppermute | solution.py:47
  83.1 6.4 %collective-permute-start.2 = (f32[3,40,4,128]{3,2,1,0:T(4,128)S(1)}, f32[3,40,4,128]{3,2,1,0:T(4,128)S(1)}, u32[]{:S(2)}, u32[]{:S(2)}) collective-permute-start(f32[3,40,4,128]{3,2,1,0:T(4,128)S(1)} %get-tuple-element.8), channel_id=1, source_target_pairs={{0,1},{1,2},{2,3},{3,4},{4,5},{5,6},{6,7},{7,8},{8,9},{9,10},{10,1... | collective-permute-start | bytes 737288 | tf_op jit(solution)/shard_map/ppermute | solution.py:45
  89.5 1.9 collective-permute-start.3
  91.5 1.1 collective-permute-done.2
  92.7 7.1 %collective-permute-done.3 = f32[3,40,4,128]{3,2,1,0:T(4,128)S(1)} collective-permute-done((f32[3,40,4,128]{3,2,1,0:T(4,128)S(1)}, f32[3,40,4,128]{3,2,1,0:T(4,128)S(1)}, u32[]{:S(2)}, u32[]{:S(2)}) %collective-permute-start.3) | collective-permute-done | bytes 245792 | tf_op jit(solution)/shard_map/ppermute | solution.py:47
  99.8 0.4 fusion.3
  100.3 1.0 fusion.21
  101.3 0.9 fusion.29
  102.2 0.9 fusion.37
  103.1 0.9 fusion.45
  104.1 2.1 collective-permute-start.6
  106.2 6.7 %collective-permute-start.7 = (f32[32,1,128]{2,1,0:T(1,128)S(1)}, f32[32,1,128]{2,1,0:T(1,128)S(1)}, u32[]{:S(2)}, u32[]{:S(2)}) collective-permute-start(f32[32,1,128]{2,1,0:T(1,128)S(1)} %get-tuple-element.20), channel_id=1, source_target_pairs={{0,1},{1,2},{2,3},{3,4},{4,5},{5,6},{6,7},{7,8},{8,9},{9,10},{10,1... | collective-permute-start | bytes 49160 | tf_op jit(solution)/shard_map/ppermute | solution.py:25
  112.9 1.9 collective-permute-start.4
  114.8 4.9 %collective-permute-start.5 = (f32[1,32,128]{2,1,0:T(8,128)S(1)}, f32[1,32,128]{2,1,0:T(8,128)S(1)}, u32[]{:S(2)}, u32[]{:S(2)}) collective-permute-start(f32[1,32,128]{2,1,0:T(8,128)S(1)} %get-tuple-element.18), channel_id=1, source_target_pairs={{0,32},{32,64},{64,96},{96,128},{128,160},{160,192},{192,224},{224... | collective-permute-start | bytes 49160 | tf_op jit(solution)/shard_map/ppermute | solution.py:25
  119.7 2.0 collective-permute-start.11
  121.8 0.6 select_maximum_fusion.4
  122.4 0.4 fusion.88
  122.8 34.9 %reshape.24 = f32[16,2,16,2,64,2]{5,4,3,2,1,0:T(8,128)} reshape(f32[32,32,128]{2,1,0:T(8,128)S(1)} %fusion.88) | data formatting | bytes 1048576 | tf_op jit(solution)/shard_map/reshape | solution.py:126
  157.7 12.2 %reduce_sum.19 = f32[16,16,64]{2,1,0:T(8,128)S(1)} reduce(f32[16,2,16,2,64,2]{5,4,3,2,1,0:T(8,128)} %reshape.24, f32[]{:T(128)} %constant.88.clone.1), dimensions={1,3,5}, to_apply=%region_5.6 | reduce | flops 114688 | bytes 589828 | tf_op jit(solution)/shard_map/reduce_sum | solution.py:126
  169.9 1.9 collective-permute-start.8
  171.9 3.4 %collective-permute-start.9 = (f32[16,4,64]{2,1,0:T(4,128)S(1)}, f32[16,4,64]{2,1,0:T(4,128)S(1)}, u32[]{:S(2)}, u32[]{:S(2)}) collective-permute-start(f32[16,4,64]{2,1,0:T(4,128)S(1)} %get-tuple-element.35), channel_id=1, source_target_pairs={{1,0},{2,1},{3,2},{4,3},{5,4},{6,5},{7,6},{8,7},{9,8},{10,9},{11,1... | collective-permute-start | bytes 49160 | tf_op jit(solution)/shard_map/ppermute | solution.py:47
  175.4 4.4 %collective-permute-done.9 = f32[16,4,64]{2,1,0:T(4,128)S(1)} collective-permute-done((f32[16,4,64]{2,1,0:T(4,128)S(1)}, f32[16,4,64]{2,1,0:T(4,128)S(1)}, u32[]{:S(2)}, u32[]{:S(2)}) %collective-permute-start.9) | collective-permute-done | bytes 16416 | tf_op jit(solution)/shard_map/ppermute | solution.py:47
  180.1 3.8 %collective-permute-start.12 = (f32[1,24,64]{2,1,0:T(8,128)S(1)}, f32[1,24,64]{2,1,0:T(8,128)S(1)}, u32[]{:S(2)}, u32[]{:S(2)}) collective-permute-start(f32[1,24,64]{2,1,0:T(8,128)S(1)} %get-tuple-element.33), channel_id=1, source_target_pairs={{32,0},{64,32},{96,64},{128,96},{160,128},{192,160},{224,192},{256... | collective-permute-start | bytes 18440 | tf_op jit(solution)/shard_map/ppermute | solution.py:47
  183.9 3.7 %collective-permute-start.13 = (f32[1,24,64]{2,1,0:T(8,128)S(1)}, f32[1,24,64]{2,1,0:T(8,128)S(1)}, u32[]{:S(2)}, u32[]{:S(2)}) collective-permute-start(f32[1,24,64]{2,1,0:T(8,128)S(1)} %get-tuple-element.32), channel_id=1, source_target_pairs={{0,32},{32,64},{64,96},{96,128},{128,160},{160,192},{192,224},{224... | collective-permute-start | bytes 18440 | tf_op jit(solution)/shard_map/ppermute | solution.py:45
  187.6 0.8 collective-permute-done.13
  188.9 2.4 collective-permute-start.14
  191.3 4.9 %collective-permute-start.15 = (f32[1,24,64]{2,1,0:T(8,128)S(1)}, f32[1,24,64]{2,1,0:T(8,128)S(1)}, u32[]{:S(2)}, u32[]{:S(2)}) collective-permute-start(f32[1,24,64]{2,1,0:T(8,128)S(1)} %get-tuple-element.30), channel_id=1, source_target_pairs={{0,32},{32,64},{64,96},{96,128},{128,160},{160,192},{192,224},{224... | collective-permute-start | bytes 18440 | tf_op jit(solution)/shard_map/ppermute | solution.py:45
  196.2 0.8 collective-permute-done.15
  197.2 0.3 fusion.111
  197.5 1.9 collective-permute-start.16
  199.4 5.6 %collective-permute-start.17 = (f32[1,24,64]{2,1,0:T(8,128)S(1)}, f32[1,24,64]{2,1,0:T(8,128)S(1)}, u32[]{:S(2)}, u32[]{:S(2)}) collective-permute-start(f32[1,24,64]{2,1,0:T(8,128)S(1)} %get-tuple-element.26), channel_id=1, source_target_pairs={{0,32},{32,64},{64,96},{96,128},{128,160},{160,192},{192,224},{224... | collective-permute-start | bytes 18440 | tf_op jit(solution)/shard_map/ppermute | solution.py:45
  205.2 0.4 collective-permute-done.17
  206.1 11.4 %broadcast_in_dim.20 = f32[16,2,16,2,64,2]{5,4,3,2,1,0:T(8,128)} broadcast(f32[16,16,64]{2,1,0:T(8,128)S(1)} %slice_select_fusion), dimensions={0,2,4} | broadcast | bytes 589824 | tf_op jit(solution)/shard_map/broadcast_in_dim | solution.py:66
  217.5 24.0 %reshape.25 = f32[32,32,128]{2,1,0:T(8,128)S(1)} reshape(f32[16,2,16,2,64,2]{5,4,3,2,1,0:T(8,128)} %broadcast_in_dim.20) | data formatting | bytes 1048576 | tf_op jit(solution)/shard_map/reshape | solution.py:69
  241.8 5.4 %collective-permute-start.18 = (f32[3,4,32,128]{3,2,1,0:T(8,128)S(1)}, f32[3,4,32,128]{3,2,1,0:T(8,128)S(1)}, u32[]{:S(2)}, u32[]{:S(2)}) collective-permute-start(f32[3,4,32,128]{3,2,1,0:T(8,128)S(1)} %get-tuple-element.10), channel_id=1, source_target_pairs={{0,32},{32,64},{64,96},{96,128},{128,160},{160,192},{192,224},{224... | collective-permute-start | bytes 589832 | tf_op jit(solution)/shard_map/ppermute | solution.py:45
  247.2 1.9 collective-permute-start.19
  249.1 0.7 collective-permute-done.18
  249.8 5.6 %collective-permute-done.19 = f32[3,4,32,128]{3,2,1,0:T(8,128)S(1)} collective-permute-done((f32[3,4,32,128]{3,2,1,0:T(8,128)S(1)}, f32[3,4,32,128]{3,2,1,0:T(8,128)S(1)}, u32[]{:S(2)}, u32[]{:S(2)}) %collective-permute-start.19) | collective-permute-done | bytes 196640 | tf_op jit(solution)/shard_map/ppermute | solution.py:47
  255.7 1.9 collective-permute-start.20
  257.6 3.4 %collective-permute-start.21 = (f32[3,40,4,128]{3,2,1,0:T(4,128)S(1)}, f32[3,40,4,128]{3,2,1,0:T(4,128)S(1)}, u32[]{:S(2)}, u32[]{:S(2)}) collective-permute-start(f32[3,40,4,128]{3,2,1,0:T(4,128)S(1)} %get-tuple-element.7), channel_id=1, source_target_pairs={{1,0},{2,1},{3,2},{4,3},{5,4},{6,5},{7,6},{8,7},{9,8},{10,9},{11,1... | collective-permute-start | bytes 737288 | tf_op jit(solution)/shard_map/ppermute | solution.py:47
  261.0 1.9 collective-permute-done.20
  262.9 5.0 %collective-permute-done.21 = f32[3,40,4,128]{3,2,1,0:T(4,128)S(1)} collective-permute-done((f32[3,40,4,128]{3,2,1,0:T(4,128)S(1)}, f32[3,40,4,128]{3,2,1,0:T(4,128)S(1)}, u32[]{:S(2)}, u32[]{:S(2)}) %collective-permute-start.21) | collective-permute-done | bytes 245792 | tf_op jit(solution)/shard_map/ppermute | solution.py:47
  267.9 0.4 fusion.7
  268.3 1.1 fusion.53
  269.4 1.0 fusion.61
  270.4 1.0 fusion.69
  271.4 0.9 fusion.77
  272.3 1.9 collective-permute-start.24
  274.3 6.7 %collective-permute-start.25 = (f32[32,1,128]{2,1,0:T(1,128)S(1)}, f32[32,1,128]{2,1,0:T(1,128)S(1)}, u32[]{:S(2)}, u32[]{:S(2)}) collective-permute-start(f32[32,1,128]{2,1,0:T(1,128)S(1)} %get-tuple-element.16), channel_id=1, source_target_pairs={{0,1},{1,2},{2,3},{3,4},{4,5},{5,6},{6,7},{7,8},{8,9},{9,10},{10,1... | collective-permute-start | bytes 49160 | tf_op jit(solution)/shard_map/ppermute | solution.py:25
  281.0 1.9 collective-permute-start.22
  282.9 4.9 %collective-permute-start.23 = (f32[1,32,128]{2,1,0:T(8,128)S(1)}, f32[1,32,128]{2,1,0:T(8,128)S(1)}, u32[]{:S(2)}, u32[]{:S(2)}) collective-permute-start(f32[1,32,128]{2,1,0:T(8,128)S(1)} %get-tuple-element.14), channel_id=1, source_target_pairs={{0,32},{32,64},{64,96},{96,128},{128,160},{160,192},{192,224},{224... | collective-permute-start | bytes 49160 | tf_op jit(solution)/shard_map/ppermute | solution.py:25
  287.9 0.7 collective-permute-done.23
  288.6 0.6 select_maximum_fusion
  289.2 1.2 fusion.83
  (64 shorter events, 3.3 us)
Async XLA Ops:
  0.6 64.1 %copy-start.2 = (f32[32,32,128]{2,1,0:T(8,128)S(1)}, f32[32,32,128]{2,1,0:T(8,128)}, u32[]{:S(2)}) copy-start(f32[32,32,128]{2,1,0:T(8,128)} %param.4) | copy-start | bytes 1572868
  64.9 13.6 %collective-permute-start = (f32[3,4,32,128]{3,2,1,0:T(8,128)S(1)}, f32[3,4,32,128]{3,2,1,0:T(8,128)S(1)}, u32[]{:S(2)}, u32[]{:S(2)}) collective-permute-start(f32[3,4,32,128]{3,2,1,0:T(8,128)S(1)} %get-tuple-element.12), channel_id=1, source_target_pairs={{0,32},{32,64},{64,96},{96,128},{128,160},{160,192},{192,224},{224... | collective-permute-start | bytes 589832 | tf_op jit(solution)/shard_map/ppermute | solution.py:45
  74.6 8.2 %collective-permute-start.1 = (f32[3,4,32,128]{3,2,1,0:T(8,128)S(1)}, f32[3,4,32,128]{3,2,1,0:T(8,128)S(1)}, u32[]{:S(2)}, u32[]{:S(2)}) collective-permute-start(f32[3,4,32,128]{3,2,1,0:T(8,128)S(1)} %get-tuple-element.13), channel_id=1, source_target_pairs={{32,0},{64,32},{96,64},{128,96},{160,128},{192,160},{224,192},{256... | collective-permute-start | bytes 589832 | tf_op jit(solution)/shard_map/ppermute | solution.py:47
  76.6 98.7 %collective-permute-start.10 = (f32[1,24,64]{2,1,0:T(8,128)S(1)}, f32[1,24,64]{2,1,0:T(8,128)S(1)}, u32[]{:S(2)}, u32[]{:S(2)}) collective-permute-start(f32[1,24,64]{2,1,0:T(8,128)S(1)} %broadcast.124), channel_id=1, source_target_pairs={{32,0},{64,32},{96,64},{128,96},{160,128},{192,160},{224,192},{256... | collective-permute-start | bytes 18440 | tf_op jit(solution)/shard_map/ppermute | solution.py:47
  83.1 9.6 %collective-permute-start.2 = (f32[3,40,4,128]{3,2,1,0:T(4,128)S(1)}, f32[3,40,4,128]{3,2,1,0:T(4,128)S(1)}, u32[]{:S(2)}, u32[]{:S(2)}) collective-permute-start(f32[3,40,4,128]{3,2,1,0:T(4,128)S(1)} %get-tuple-element.8), channel_id=1, source_target_pairs={{0,1},{1,2},{2,3},{3,4},{4,5},{5,6},{6,7},{7,8},{8,9},{9,10},{10,1... | collective-permute-start | bytes 737288 | tf_op jit(solution)/shard_map/ppermute | solution.py:45
  89.5 10.3 %collective-permute-start.3 = (f32[3,40,4,128]{3,2,1,0:T(4,128)S(1)}, f32[3,40,4,128]{3,2,1,0:T(4,128)S(1)}, u32[]{:S(2)}, u32[]{:S(2)}) collective-permute-start(f32[3,40,4,128]{3,2,1,0:T(4,128)S(1)} %get-tuple-element.9), channel_id=1, source_target_pairs={{1,0},{2,1},{3,2},{4,3},{5,4},{6,5},{7,6},{8,7},{9,8},{10,9},{11,1... | collective-permute-start | bytes 737288 | tf_op jit(solution)/shard_map/ppermute | solution.py:47
  104.0 18.3 %copy-start = (f32[32,32,128]{2,1,0:T(8,128)S(1)}, f32[32,32,128]{2,1,0:T(8,128)}, u32[]{:S(2)}) copy-start(f32[32,32,128]{2,1,0:T(8,128)} %param.3) | copy-start | bytes 1572868
  104.1 15.6 %collective-permute-start.6 = (f32[32,1,128]{2,1,0:T(1,128)S(1)}, f32[32,1,128]{2,1,0:T(1,128)S(1)}, u32[]{:S(2)}, u32[]{:S(2)}) collective-permute-start(f32[32,1,128]{2,1,0:T(1,128)S(1)} %get-tuple-element.21), channel_id=1, source_target_pairs={{1,0},{2,1},{3,2},{4,3},{5,4},{6,5},{7,6},{8,7},{9,8},{10,9},{11,1... | collective-permute-start | bytes 49160 | tf_op jit(solution)/shard_map/ppermute | solution.py:26
  106.2 15.6 %collective-permute-start.7 = (f32[32,1,128]{2,1,0:T(1,128)S(1)}, f32[32,1,128]{2,1,0:T(1,128)S(1)}, u32[]{:S(2)}, u32[]{:S(2)}) collective-permute-start(f32[32,1,128]{2,1,0:T(1,128)S(1)} %get-tuple-element.20), channel_id=1, source_target_pairs={{0,1},{1,2},{2,3},{3,4},{4,5},{5,6},{6,7},{7,8},{8,9},{9,10},{10,1... | collective-permute-start | bytes 49160 | tf_op jit(solution)/shard_map/ppermute | solution.py:25
  112.9 8.9 %collective-permute-start.4 = (f32[1,32,128]{2,1,0:T(8,128)S(1)}, f32[1,32,128]{2,1,0:T(8,128)S(1)}, u32[]{:S(2)}, u32[]{:S(2)}) collective-permute-start(f32[1,32,128]{2,1,0:T(8,128)S(1)} %get-tuple-element.19), channel_id=1, source_target_pairs={{32,0},{64,32},{96,64},{128,96},{160,128},{192,160},{224,192},{256... | collective-permute-start | bytes 49160 | tf_op jit(solution)/shard_map/ppermute | solution.py:26
  114.8 7.0 %collective-permute-start.5 = (f32[1,32,128]{2,1,0:T(8,128)S(1)}, f32[1,32,128]{2,1,0:T(8,128)S(1)}, u32[]{:S(2)}, u32[]{:S(2)}) collective-permute-start(f32[1,32,128]{2,1,0:T(8,128)S(1)} %get-tuple-element.18), channel_id=1, source_target_pairs={{0,32},{32,64},{64,96},{96,128},{128,160},{160,192},{192,224},{224... | collective-permute-start | bytes 49160 | tf_op jit(solution)/shard_map/ppermute | solution.py:25
  119.7 55.5 %collective-permute-start.11 = (f32[1,24,64]{2,1,0:T(8,128)S(1)}, f32[1,24,64]{2,1,0:T(8,128)S(1)}, u32[]{:S(2)}, u32[]{:S(2)}) collective-permute-start(f32[1,24,64]{2,1,0:T(8,128)S(1)} %broadcast.124), channel_id=1, source_target_pairs={{0,32},{32,64},{64,96},{96,128},{128,160},{160,192},{192,224},{224... | collective-permute-start | bytes 18440 | tf_op jit(solution)/shard_map/ppermute | solution.py:45
  169.9 5.5 %collective-permute-start.8 = (f32[16,4,64]{2,1,0:T(4,128)S(1)}, f32[16,4,64]{2,1,0:T(4,128)S(1)}, u32[]{:S(2)}, u32[]{:S(2)}) collective-permute-start(f32[16,4,64]{2,1,0:T(4,128)S(1)} %get-tuple-element.34), channel_id=1, source_target_pairs={{0,1},{1,2},{2,3},{3,4},{4,5},{5,6},{6,7},{7,8},{8,9},{9,10},{10,1... | collective-permute-start | bytes 49160 | tf_op jit(solution)/shard_map/ppermute | solution.py:45
  171.9 8.0 %collective-permute-start.9 = (f32[16,4,64]{2,1,0:T(4,128)S(1)}, f32[16,4,64]{2,1,0:T(4,128)S(1)}, u32[]{:S(2)}, u32[]{:S(2)}) collective-permute-start(f32[16,4,64]{2,1,0:T(4,128)S(1)} %get-tuple-element.35), channel_id=1, source_target_pairs={{1,0},{2,1},{3,2},{4,3},{5,4},{6,5},{7,6},{8,7},{9,8},{10,9},{11,1... | collective-permute-start | bytes 49160 | tf_op jit(solution)/shard_map/ppermute | solution.py:47
  180.1 7.5 %collective-permute-start.12 = (f32[1,24,64]{2,1,0:T(8,128)S(1)}, f32[1,24,64]{2,1,0:T(8,128)S(1)}, u32[]{:S(2)}, u32[]{:S(2)}) collective-permute-start(f32[1,24,64]{2,1,0:T(8,128)S(1)} %get-tuple-element.33), channel_id=1, source_target_pairs={{32,0},{64,32},{96,64},{128,96},{160,128},{192,160},{224,192},{256... | collective-permute-start | bytes 18440 | tf_op jit(solution)/shard_map/ppermute | solution.py:47
  183.9 4.5 %collective-permute-start.13 = (f32[1,24,64]{2,1,0:T(8,128)S(1)}, f32[1,24,64]{2,1,0:T(8,128)S(1)}, u32[]{:S(2)}, u32[]{:S(2)}) collective-permute-start(f32[1,24,64]{2,1,0:T(8,128)S(1)} %get-tuple-element.32), channel_id=1, source_target_pairs={{0,32},{32,64},{64,96},{96,128},{128,160},{160,192},{192,224},{224... | collective-permute-start | bytes 18440 | tf_op jit(solution)/shard_map/ppermute | solution.py:45
  188.9 7.3 %collective-permute-start.14 = (f32[1,24,64]{2,1,0:T(8,128)S(1)}, f32[1,24,64]{2,1,0:T(8,128)S(1)}, u32[]{:S(2)}, u32[]{:S(2)}) collective-permute-start(f32[1,24,64]{2,1,0:T(8,128)S(1)} %get-tuple-element.31), channel_id=1, source_target_pairs={{32,0},{64,32},{96,64},{128,96},{160,128},{192,160},{224,192},{256... | collective-permute-start | bytes 18440 | tf_op jit(solution)/shard_map/ppermute | solution.py:47
  191.3 5.7 %collective-permute-start.15 = (f32[1,24,64]{2,1,0:T(8,128)S(1)}, f32[1,24,64]{2,1,0:T(8,128)S(1)}, u32[]{:S(2)}, u32[]{:S(2)}) collective-permute-start(f32[1,24,64]{2,1,0:T(8,128)S(1)} %get-tuple-element.30), channel_id=1, source_target_pairs={{0,32},{32,64},{64,96},{96,128},{128,160},{160,192},{192,224},{224... | collective-permute-start | bytes 18440 | tf_op jit(solution)/shard_map/ppermute | solution.py:45
  197.5 7.7 %collective-permute-start.16 = (f32[1,24,64]{2,1,0:T(8,128)S(1)}, f32[1,24,64]{2,1,0:T(8,128)S(1)}, u32[]{:S(2)}, u32[]{:S(2)}) collective-permute-start(f32[1,24,64]{2,1,0:T(8,128)S(1)} %get-tuple-element.27), channel_id=1, source_target_pairs={{32,0},{64,32},{96,64},{128,96},{160,128},{192,160},{224,192},{256... | collective-permute-start | bytes 18440 | tf_op jit(solution)/shard_map/ppermute | solution.py:47
  199.4 6.2 %collective-permute-start.17 = (f32[1,24,64]{2,1,0:T(8,128)S(1)}, f32[1,24,64]{2,1,0:T(8,128)S(1)}, u32[]{:S(2)}, u32[]{:S(2)}) collective-permute-start(f32[1,24,64]{2,1,0:T(8,128)S(1)} %get-tuple-element.26), channel_id=1, source_target_pairs={{0,32},{32,64},{64,96},{96,128},{128,160},{160,192},{192,224},{224... | collective-permute-start | bytes 18440 | tf_op jit(solution)/shard_map/ppermute | solution.py:45
  241.8 8.0 %collective-permute-start.18 = (f32[3,4,32,128]{3,2,1,0:T(8,128)S(1)}, f32[3,4,32,128]{3,2,1,0:T(8,128)S(1)}, u32[]{:S(2)}, u32[]{:S(2)}) collective-permute-start(f32[3,4,32,128]{3,2,1,0:T(8,128)S(1)} %get-tuple-element.10), channel_id=1, source_target_pairs={{0,32},{32,64},{64,96},{96,128},{128,160},{160,192},{192,224},{224... | collective-permute-start | bytes 589832 | tf_op jit(solution)/shard_map/ppermute | solution.py:45
  247.2 8.2 %collective-permute-start.19 = (f32[3,4,32,128]{3,2,1,0:T(8,128)S(1)}, f32[3,4,32,128]{3,2,1,0:T(8,128)S(1)}, u32[]{:S(2)}, u32[]{:S(2)}) collective-permute-start(f32[3,4,32,128]{3,2,1,0:T(8,128)S(1)} %get-tuple-element.11), channel_id=1, source_target_pairs={{32,0},{64,32},{96,64},{128,96},{160,128},{192,160},{224,192},{256... | collective-permute-start | bytes 589832 | tf_op jit(solution)/shard_map/ppermute | solution.py:47
  255.7 7.2 %collective-permute-start.20 = (f32[3,40,4,128]{3,2,1,0:T(4,128)S(1)}, f32[3,40,4,128]{3,2,1,0:T(4,128)S(1)}, u32[]{:S(2)}, u32[]{:S(2)}) collective-permute-start(f32[3,40,4,128]{3,2,1,0:T(4,128)S(1)} %get-tuple-element.6), channel_id=1, source_target_pairs={{0,1},{1,2},{2,3},{3,4},{4,5},{5,6},{6,7},{7,8},{8,9},{9,10},{10,1... | collective-permute-start | bytes 737288 | tf_op jit(solution)/shard_map/ppermute | solution.py:45
  257.6 10.3 %collective-permute-start.21 = (f32[3,40,4,128]{3,2,1,0:T(4,128)S(1)}, f32[3,40,4,128]{3,2,1,0:T(4,128)S(1)}, u32[]{:S(2)}, u32[]{:S(2)}) collective-permute-start(f32[3,40,4,128]{3,2,1,0:T(4,128)S(1)} %get-tuple-element.7), channel_id=1, source_target_pairs={{1,0},{2,1},{3,2},{4,3},{5,4},{6,5},{7,6},{8,7},{9,8},{10,9},{11,1... | collective-permute-start | bytes 737288 | tf_op jit(solution)/shard_map/ppermute | solution.py:47
  272.3 15.5 %collective-permute-start.24 = (f32[32,1,128]{2,1,0:T(1,128)S(1)}, f32[32,1,128]{2,1,0:T(1,128)S(1)}, u32[]{:S(2)}, u32[]{:S(2)}) collective-permute-start(f32[32,1,128]{2,1,0:T(1,128)S(1)} %get-tuple-element.17), channel_id=1, source_target_pairs={{1,0},{2,1},{3,2},{4,3},{5,4},{6,5},{7,6},{8,7},{9,8},{10,9},{11,1... | collective-permute-start | bytes 49160 | tf_op jit(solution)/shard_map/ppermute | solution.py:26
  274.3 13.6 %collective-permute-start.25 = (f32[32,1,128]{2,1,0:T(1,128)S(1)}, f32[32,1,128]{2,1,0:T(1,128)S(1)}, u32[]{:S(2)}, u32[]{:S(2)}) collective-permute-start(f32[32,1,128]{2,1,0:T(1,128)S(1)} %get-tuple-element.16), channel_id=1, source_target_pairs={{0,1},{1,2},{2,3},{3,4},{4,5},{5,6},{6,7},{7,8},{8,9},{9,10},{10,1... | collective-permute-start | bytes 49160 | tf_op jit(solution)/shard_map/ppermute | solution.py:25
  281.0 6.9 %collective-permute-start.22 = (f32[1,32,128]{2,1,0:T(8,128)S(1)}, f32[1,32,128]{2,1,0:T(8,128)S(1)}, u32[]{:S(2)}, u32[]{:S(2)}) collective-permute-start(f32[1,32,128]{2,1,0:T(8,128)S(1)} %get-tuple-element.15), channel_id=1, source_target_pairs={{32,0},{64,32},{96,64},{128,96},{160,128},{192,160},{224,192},{256... | collective-permute-start | bytes 49160 | tf_op jit(solution)/shard_map/ppermute | solution.py:26
  282.9 5.7 %collective-permute-start.23 = (f32[1,32,128]{2,1,0:T(8,128)S(1)}, f32[1,32,128]{2,1,0:T(8,128)S(1)}, u32[]{:S(2)}, u32[]{:S(2)}) collective-permute-start(f32[1,32,128]{2,1,0:T(8,128)S(1)} %get-tuple-element.14), channel_id=1, source_target_pairs={{0,32},{32,64},{64,96},{96,128},{128,160},{160,192},{192,224},{224... | collective-permute-start | bytes 49160 | tf_op jit(solution)/shard_map/ppermute | solution.py:25
  287.8 2.6 copy-start.1
where the time goes:
time: 292 us; the launch traced here: 290 us
  starting transfers between devices  95 us (33%)
  local copies, waits for them, and re-layouts  71.1 us (24%)
  blocking collectives  59.6 us (20%)
  waiting for transfers between devices  32.9 us (11%)
  other arithmetic  29.7 us (10%)
    psum x4, blocking collectives, by_axis(): return functools.reduce(lax.psum, axes, shard)  59.6 us
    ppermute x9, starting transfers between devices, with_halo(): lax.ppermute(tail, axis, [(i, (i + 1) % count) for i in range(ends)])  41.6 us
    reshape x1, local copies, waits for them, and re-layouts, per_device(): fine_residual.reshape(half_x, 2, half_y, 2, half_z, 2).sum(axis=(1, 3, 5))  34.9 us
    ppermute x9, waiting for transfers between devices, with_halo(): lax.ppermute(head, axis, [((i + 1) % count, i) for i in range(ends)])  26.4 us
    reshape x1, local copies, waits for them, and re-layouts, expand(): return wide.reshape(size_a * factor, size_b * factor, size_c * factor)  24 us
    ppermute x4, starting transfers between devices, extended(): lax.ppermute(last, axis, up)  23.1 us
    ppermute x9, starting transfers between devices, with_halo(): lax.ppermute(head, axis, [((i + 1) % count, i) for i in range(ends)])  22.5 us
    reduce_sum x1, other arithmetic, per_device(): fine_residual.reshape(half_x, 2, half_y, 2, half_z, 2).sum(axis=(1, 3, 5))  12.2 us
  transfers between devices with their start and end apart: 26, of which 12 were waited for; matrix products, arithmetic and copies ran while one was open for 18% of the time, Pallas kernels for 0%

commit v1 on v0

v1 whole, which is shorter than its diff:
```python
import jax
import jax.numpy as jnp
from jax import lax
from jax.experimental import pallas as pl
from jax.experimental.pallas import tpu as pltpu
from jax.sharding import PartitionSpec as P

GROUP = "group"
MEMBER = "member"
N = 32
NZ = 128
K = N // 2
H = 16
KH = H // 2
NX = N + 2 * H
NK = K + 2 * KH
PAD = 8
SIXTH = 1.0 / 6.0
F32 = jnp.float32
LIMIT = 40 * 1024 * 1024


def lanes(rows):
    return lax.broadcasted_iota(jnp.int32, (rows, NZ), 1)


def rows_of(rows):
    return lax.broadcasted_iota(jnp.int32, (rows, NZ), 0)


def split(ref, x, first):
    even = ref[x, pl.ds(0, K, stride=2), :]
    odd = ref[x, pl.ds(1, K, stride=2), :]
    return jnp.where(first, even, odd), jnp.where(first, odd, even)


def box_flags(refined, rows):
    z = lanes(rows)
    out = jnp.zeros((rows, NZ), F32)
    for b in range(NZ // N):
        on = jnp.where(refined[0, 0, b] == 1, 1.0, 0.0).astype(F32)
        out = jnp.where(z // N == b, on, out)
    return out


def pack_kernel(source, potential, refined, up, down, part):
    zp = lanes(K) % 2
    row = rows_of(8)
    zp8 = lanes(8) % 2

    def body(i, acc):
        for j in range(2):
            x = 2 * i + j
            first = zp == j
            pr, pb = split(potential, x, first)
            sr, sb = split(source, x, first)
            acc = acc + (sr + sb)
            up[x] = pr[KH:]
            down[x] = pr[:KH]
            up[N + x] = pb[KH:]
            down[N + x] = pb[:KH]
            beyond_up = jnp.where((row == 0) & (zp8 == j), pltpu.roll(pb[:KH], 1, 0), 0.0)
            beyond_down = jnp.where((row == KH - 1) & (zp8 != j), pltpu.roll(pb[KH:], KH - 1, 0), 0.0)
            up[2 * N + x] = sr[KH:] + beyond_up
            down[2 * N + x] = sr[:KH] + beyond_down
            up[3 * N + x] = sb[KH:]
            down[3 * N + x] = sb[:KH]
        return acc

    acc = lax.fori_loop(0, N // 2, body, jnp.zeros((K, NZ), F32))
    part[...] = jnp.broadcast_to(jnp.sum(acc, axis=0, keepdims=True), part.shape)
    flags = box_flags(refined, 8)
    up[4 * N] = flags
    down[4 * N] = flags


def middle_kernel(source, potential, refined, low, high, parts, up, down, wide, part):
    zp = lanes(K) % 2

    def put(ref, at, x, a, own):
        ref[at, :KH] = low[a * N + x]
        ref[at, KH : KH + K] = own
        ref[at, KH + K :] = high[a * N + x]

    for half, msg in ((0, down), (1, up)):

        def body(i, carry, half=half, msg=msg):
            for j in range(2):
                xh = 2 * i + j
                x = xh + half * H
                first = zp == j
                fields = split(potential, x, first) + split(source, x, first)
                for a in range(4):
                    put(wide, a * N + x, x, a, fields[a])
                    put(msg, a * H + xh, x, a, fields[a])
            return carry

        lax.fori_loop(0, H // 2, body, 0)
    up[2 * H] = up[2 * H] + wide[N + H - 1]
    down[3 * H - 1] = down[3 * H - 1] + wide[N + H]
    flags = box_flags(refined, K)
    for ref, at in ((up, 4 * H), (down, 4 * H), (wide, 4 * N)):
        ref[at, :KH] = low[4 * N]
        ref[at, KH : KH + K] = flags
        ref[at, KH + K :] = high[4 * N]
    part[...] = jnp.broadcast_to(jnp.sum(parts[...], axis=0, keepdims=True), part.shape)


def neighbours(ref, x, r0, rows, here, below_first, z):
    centre = ref[x, r0 : r0 + rows, :]
    below = ref[x, r0 - 1 : r0 - 1 + rows, :]
    above = ref[x, r0 + 1 : r0 + 1 + rows, :]
    side = jnp.where(here, below, above) if below_first else jnp.where(here, above, below)
    left = jnp.where(z == 0, 0.0, pltpu.roll(centre, 1, 1))
    right = jnp.where(z == NZ - 1, 0.0, pltpu.roll(centre, NZ - 1, 1))
    along_x = ref[x - 1, r0 : r0 + rows, :] + ref[x + 1, r0 : r0 + rows, :]
    return (along_x + (centre + side)) + (left + right)


def half_sweep(dst, src, rhs, masks, colour, x_from, x_to, row_from, rows):
    z = lanes(rows)
    zp = z % 2
    r0 = PAD + row_from

    def body(i, carry):
        base = x_from + 4 * i
        on = masks[base // H, row_from : row_from + rows, :] > 0.5
        for j in range(4):
            x = base + j
            total = neighbours(src, x + 1, r0, rows, zp == j % 2, colour == 0, z)
            update = rhs[x, row_from : row_from + rows, :] + total * SIXTH
            dst[x + 1, r0 : r0 + rows, :] = jnp.where(on, update, dst[x + 1, r0 : r0 + rows, :])
        return carry

    lax.fori_loop(0, (x_to - x_from) // 4, body, 0)


def cycle_kernel(wide, low, high, parts, place, smoothed, residual, red, black, rhs_r, rhs_b, masks, coarse, corr):
    cells = place[2] * place[3] * (N * N * NZ)
    mean = jnp.sum(parts[...]) / cells.astype(F32)

    spare = jnp.zeros((PAD, NZ), F32)
    for ref in (red, black):
        for x in (0, NX + 1):
            ref[x] = jnp.zeros((NK + 2 * PAD, NZ), F32)
    for part, start, count in ((low, 0, H), (wide, H, N), (high, H + N, H)):

        def body(i, carry, part=part, start=start, count=count):
            x = start + i
            for a, ref in ((0, red), (1, black)):
                ref[x + 1, :PAD, :] = spare
                ref[x + 1, PAD : PAD + NK, :] = part[a * count + i]
                ref[x + 1, PAD + NK :, :] = spare
            rhs_r[x] = (part[2 * count + i] - mean) * SIXTH
            rhs_b[x] = (part[3 * count + i] - mean) * SIXTH
            return carry

        lax.fori_loop(0, count, body, 0, unroll=2)
    masks[0] = low[4 * H]
    masks[1] = wide[4 * N]
    masks[2] = wide[4 * N]
    masks[3] = high[4 * H]

    for _ in range(2):
        half_sweep(red, black, rhs_r, masks, 0, 0, NX, 0, NK)
        half_sweep(black, red, rhs_b, masks, 1, 0, NX, 0, NK)

    z = lanes(NK)
    zp = z % 2

    def restrict(cx, carry):
        total = jnp.zeros((NK, NZ), F32)
        for j in range(2):
            x = 2 * cx + j
            here = zp == j
            r = slice(PAD, PAD + NK)
            nr = neighbours(black, x + 1, PAD, NK, here, True, z)
            nb = neighbours(red, x + 1, PAD, NK, here, False, z)
            gap = (rhs_r[x] - red[x + 1, r, :]) + (rhs_b[x] - black[x + 1, r, :])
            total = total + (6.0 * gap + (nr + nb))
        pair = jnp.where(zp == 0, pltpu.roll(total, NZ - 1, 1), pltpu.roll(total, 1, 1))
        coarse[cx] = (total + pair) * 0.5
        return carry

    lax.fori_loop(2, NX // 2 - 2, restrict, 0)

    row = rows_of(NK)
    global_row = place[1] * K + row - KH
    row_gain = jnp.where((global_row >= 0) & (global_row < place[3] * K), SIXTH, 0.0).astype(F32)
    parity = (row + z // 2) % 2
    for x in (0, 1, NX // 2 - 2, NX // 2 - 1):
        corr[x] = jnp.zeros((NK + 2 * PAD, NZ), F32)

    def gain_at(cx):
        at = place[0] * K + cx - KH
        return row_gain * jnp.where((at >= 0) & (at < place[2] * K), 1.0, 0.0).astype(F32)

    def start(i, carry):
        for j in range(2):
            cx = 2 * i + j
            corr[cx, :PAD, :] = spare
            corr[cx, PAD : PAD + NK, :] = jnp.where(parity == j, coarse[cx] * gain_at(cx), 0.0)
            corr[cx, PAD + NK :, :] = spare
        return carry

    lax.fori_loop(1, NX // 4 - 1, start, 0)

    def coarse_half(colour, first, last):
        def body(i, carry):
            for j in range(2):
                cx = 2 * i + j
                centre = corr[cx, PAD : PAD + NK, :]
                along_y = corr[cx, PAD - 1 : PAD - 1 + NK, :] + corr[cx, PAD + 1 : PAD + 1 + NK, :]
                along_x = corr[cx - 1, PAD : PAD + NK, :] + corr[cx + 1, PAD : PAD + NK, :]
                left = jnp.where(z < 2, 0.0, pltpu.roll(centre, 2, 1))
                right = jnp.where(z >= NZ - 2, 0.0, pltpu.roll(centre, NZ - 2, 1))
                update = (coarse[cx] + (along_x + along_y) + (left + right)) * gain_at(cx)
                corr[cx, PAD : PAD + NK, :] = jnp.where(parity == (colour + j) % 2, update, centre)
            return carry

        lax.fori_loop(first // 2, last // 2, body, 0)

    coarse_half(1, 2, 30)
    coarse_half(0, 4, 28)
    coarse_half(1, 4, 28)

    def prolong(cx, carry):
        add = corr[cx, PAD : PAD + NK, :]
        for ref in (red, black):
            for j in range(2):
                x = 2 * cx + j + 1
                ref[x, PAD : PAD + NK, :] = ref[x, PAD : PAD + NK, :] + add
        return carry

    lax.fori_loop(5, 27, prolong, 0)

    for _ in range(2):
        half_sweep(red, black, rhs_r, masks, 0, 12, 52, 4, 24)
        half_sweep(black, red, rhs_b, masks, 1, 12, 52, 4, 24)

    zk = lanes(K)
    zkp = zk % 2
    r0 = PAD + KH

    def finish(i, carry):
        for j in range(2):
            out = 2 * i + j
            x = out + H
            here = zkp == j
            r = red[x + 1, r0 : r0 + K, :]
            b = black[x + 1, r0 : r0 + K, :]
            res_r = 6.0 * (rhs_r[x, KH : KH + K, :] - r) + neighbours(black, x + 1, r0, K, here, True, zk)
            res_b = 6.0 * (rhs_b[x, KH : KH + K, :] - b) + neighbours(red, x + 1, r0, K, here, False, zk)
            for ref, one, two in ((smoothed, r, b), (residual, res_r, res_b)):
                ref[out, pl.ds(0, K, stride=2), :] = jnp.where(here, one, two)
                ref[out, pl.ds(1, K, stride=2), :] = jnp.where(here, two, one)
        return carry

    lax.fori_loop(0, N // 2, finish, 0)


def shape(*dims):
    return jax.ShapeDtypeStruct(dims, F32)


VMEM = pl.BlockSpec(memory_space=pltpu.VMEM)
SMEM = pl.BlockSpec(memory_space=pltpu.SMEM)


def call(kernel, ins, outs, scratch=()):
    return pl.pallas_call(
        kernel,
        out_shape=outs,
        in_specs=ins,
        out_specs=[VMEM] * len(outs),
        scratch_shapes=list(scratch),
        compiler_params=pltpu.CompilerParams(vmem_limit_bytes=LIMIT),
    )


def per_device(source, potential, refined):
    groups, members = lax.axis_size(GROUP), lax.axis_size(MEMBER)

    def both_ways(up, down, axis):
        size = lax.axis_size(axis)
        pairs = [(i, i + 1) for i in range(size - 1)]
        return lax.ppermute(up, axis, pairs), lax.ppermute(down, axis, [(b, a) for a, b in pairs])

    side = shape(4 * N + 1, KH, NZ)
    up, down, part = call(pack_kernel, [VMEM, VMEM, SMEM], [side, side, shape(groups, NZ)])(
        source, potential, refined
    )
    low, high = both_ways(up, down, MEMBER)
    parts = lax.all_to_all(part, GROUP, 0, 0, tiled=True)
    slab = shape(4 * H + 1, NK, NZ)
    up, down, wide, part = call(
        middle_kernel,
        [VMEM, VMEM, SMEM, VMEM, VMEM, VMEM],
        [slab, slab, shape(4 * N + 1, NK, NZ), shape(members, NZ)],
    )(source, potential, refined, low, high, parts)
    low, high = both_ways(up, down, GROUP)
    parts = lax.all_to_all(part, MEMBER, 0, 0, tiled=True)
    place = jnp.stack(
        [lax.axis_index(GROUP), lax.axis_index(MEMBER), jnp.int32(groups), jnp.int32(members)]
    ).astype(jnp.int32)
    padded = pltpu.VMEM((NX + 2, NK + 2 * PAD, NZ), F32)
    plain = pltpu.VMEM((NX, NK, NZ), F32)
    return call(
        cycle_kernel,
        [VMEM, VMEM, VMEM, VMEM, SMEM],
        [shape(N, N, NZ), shape(N, N, NZ)],
        [
            padded,
            padded,
            plain,
            plain,
            pltpu.VMEM((4, NK, NZ), F32),
            pltpu.VMEM((NX // 2, NK, NZ), F32),
            pltpu.VMEM((NX // 2, NK + 2 * PAD, NZ), F32),
        ],
    )(wide, low, high, parts, place)


def solution(mesh):
    spec = P(GROUP, MEMBER, None)
    return jax.shard_map(
        per_device, mesh=mesh, in_specs=(spec, spec, spec), out_specs=(spec, spec), check_vma=False
    )
```

time: 292 us -> 92.2 us (0.32)
  the two profiles are of different devices: /device:TPU:223 before, /device:TPU:1 now
where the time goes in v1:
time: 92.2 us; the launch traced here: 91.8 us
  blocking collectives  31.5 us (34%)
  Pallas kernels  26.6 us (29%)
  starting transfers between devices  21.8 us (24%)
  waiting for transfers between devices  8.43 us (9%)
  local copies, waits for them, and re-layouts  2.73 us (3%)
    all_to_all x1, blocking collectives, per_device(): parts = lax.all_to_all(part, GROUP, 0, 0, tiled=True)  31.5 us
    pallas_call x1, Pallas kernels, per_device(): call(cycle_kernel, [VMEM, VMEM, VMEM, VMEM, SMEM], [shape(N, N, NZ), shap...  23.7 us
    all_to_all x1, starting transfers between devices, per_device(): parts = lax.all_to_all(part, MEMBER, 0, 0, tiled=True)  11.7 us
    all_to_all x1, waiting for transfers between devices, per_device(): parts = lax.all_to_all(part, MEMBER, 0, 0, tiled=True)  8.42 us
    ppermute x2, starting transfers between devices, both_ways(): lax.ppermute(up, axis, pairs)  6.95 us
    ppermute x2, starting transfers between devices, both_ways(): lax.ppermute(down, axis, [(b, a) for a, b in pairs])  3.21 us
    unnamed x6, local copies, waits for them, and re-layouts  2.73 us
    pallas_call x1, Pallas kernels, per_device(): call(middle_kernel, [VMEM, VMEM, SMEM, VMEM, VMEM, VMEM], [slab, slab, sh...  2.2 us
  transfers between devices with their start and end apart: 5, of which 1 were waited for; matrix products, arithmetic and copies ran while one was open for 0% of the time, Pallas kernels for 0%

profile of v1, /device:TPU:1, one launch (start us, length us, event | category | flops | bytes accessed | tf_op | source)
XLA Modules:
  0.0 91.8 jit_solution(11354146768852362521)
XLA Ops:
  0.6 0.0 copy-start
  0.6 1.0 %copy-done = f32[32,32,128]{2,1,0:T(8,128)S(1)} copy-done((f32[32,32,128]{2,1,0:T(8,128)S(1)}, f32[32,32,128]{2,1,0:T(8,128)}, u32[]{:S(2)}) %copy-start) | copy-done | bytes 524312
  1.7 0.0 copy-start.1
  1.7 1.0 %copy-done.1 = f32[32,32,128]{2,1,0:T(8,128)S(1)} copy-done((f32[32,32,128]{2,1,0:T(8,128)S(1)}, f32[32,32,128]{2,1,0:T(8,128)}, u32[]{:S(2)}) %copy-start.1) | copy-done | bytes 524312
  2.7 0.0 copy-start.2
  2.7 0.7 copy-done.2
  3.4 0.7 shard_map.50
  4.1 4.0 %collective-permute-start = (f32[129,8,128]{2,1,0:T(8,128)S(1)}, f32[129,8,128]{2,1,0:T(8,128)S(1)}, u32[]{:S(2)}, u32[]{:S(2)}) collective-permute-start(f32[129,8,128]{2,1,0:T(8,128)S(1)} %get-tuple-element.9), channel_id=1, source_target_pairs={{0,1},{1,2},{2,3},{3,4},{4,5},{5,6},{6,7},{7,8},{8,9},{9,10},{10,1... | collective-permute-start | bytes 1585160 | tf_op jit(solution)/shard_map/ppermute | solution.py:287
  8.1 1.3 %collective-permute-start.1 = (f32[129,8,128]{2,1,0:T(8,128)S(1)}, f32[129,8,128]{2,1,0:T(8,128)S(1)}, u32[]{:S(2)}, u32[]{:S(2)}) collective-permute-start(f32[129,8,128]{2,1,0:T(8,128)S(1)} %get-tuple-element.10), channel_id=1, source_target_pairs={{1,0},{2,1},{3,2},{4,3},{5,4},{6,5},{7,6},{8,7},{9,8},{10,9},{11,1... | collective-permute-start | bytes 1585160 | tf_op jit(solution)/shard_map/ppermute | solution.py:287
  9.4 31.5 %all_to_all.22 = f32[32,1,128]{2,1,0:T(1,128)S(1)} all-to-all(f32[32,1,128]{2,1,0:T(1,128)S(1)} %bitcast.12), channel_id=1, replica_groups=mesh['group'=32,'member'=32] {'group'}, dimensions={0} | all-to-all | bytes 32768 | tf_op jit(solution)/shard_map/all_to_all | solution.py:294
  40.8 0.0 collective-permute-done.low
  40.8 0.0 collective-permute-done.1.high
  40.8 2.2 %shard_map.51 = (f32[65,32,128]{2,1,0:T(8,128)}, f32[65,32,128]{2,1,0:T(8,128)}, f32[129,32,128]{2,1,0:T(8,128)S(1)}, f32[32,128]{1,0:T(8,128)}) custom-call(f32[32,32,128]{2,1,0:T(8,128)S(1)} %copy-done, f32[32,32,128]{2,1,0:T(8,128)S(1)} %copy-done.1, s32[1,1,4]{2,1,0:T(1,128)S(1)} %copy-done.2, f32[129,8,128]{2,1,0:T(8,128)S(1)} %collective-permute-done.low, ...), custom_call_target="tpu_custom_call" | custom-call | tf_op jit(solution)/shard_map/pallas_call | solution.py:296
  43.0 3.0 %collective-permute-start.2 = (f32[65,32,128]{2,1,0:T(8,128)}, f32[65,32,128]{2,1,0:T(8,128)S(1)}, u32[]{:S(2)}, u32[]{:S(2)}) collective-permute-start(f32[65,32,128]{2,1,0:T(8,128)} %get-tuple-element.13), channel_id=1, source_target_pairs={{0,32},{32,64},{64,96},{96,128},{128,160},{160,192},{192,224},{224... | collective-permute-start | bytes 3194888 | tf_op jit(solution)/shard_map/ppermute | solution.py:287
  46.0 1.9 %collective-permute-start.3 = (f32[65,32,128]{2,1,0:T(8,128)}, f32[65,32,128]{2,1,0:T(8,128)}, u32[]{:S(2)}, u32[]{:S(2)}) collective-permute-start(f32[65,32,128]{2,1,0:T(8,128)} %get-tuple-element.14), channel_id=1, source_target_pairs={{32,0},{64,32},{96,64},{128,96},{160,128},{192,160},{224,192},{256... | collective-permute-start | bytes 3194888 | tf_op jit(solution)/shard_map/ppermute | solution.py:287
  47.9 11.7 %all-to-all-start.1 = ((f32[32,1,128]{2,1,0:T(1,128)}), f32[32,1,128]{2,1,0:T(1,128)S(1)}, u32[]{:S(2)}, u32[]{:S(2)}) async-start(f32[32,1,128]{2,1,0:T(1,128)} %bitcast.4), calls=%async_computation.1 | async-start | bytes 32768 | tf_op jit(solution)/shard_map/all_to_all | solution.py:302
  59.6 0.1 pad_add_fusion.place
  59.7 8.4 %all-to-all-done.1 = f32[32,1,128]{2,1,0:T(1,128)S(1)} async-done(((f32[32,1,128]{2,1,0:T(1,128)}), f32[32,1,128]{2,1,0:T(1,128)S(1)}, u32[]{:S(2)}, u32[]{:S(2)}) %all-to-all-start.1) | async-done | bytes 16416 | tf_op jit(solution)/shard_map/all_to_all | solution.py:302
  68.1 0.0 collective-permute-done.2.low
  68.1 0.0 collective-permute-done.3.high
  68.1 23.7 %shard_map.52 = (f32[32,32,128]{2,1,0:T(8,128)}, f32[32,32,128]{2,1,0:T(8,128)}) custom-call(f32[129,32,128]{2,1,0:T(8,128)S(1)} %get-tuple-element.12.wide, f32[65,32,128]{2,1,0:T(8,128)S(1)} %collective-permute-done.2.low, f32[65,32,128]{2,1,0:T(8,128)} %collective-permute-done.3.high, f32[32,128]{1,0:T(8,128)S(1)} %bitcast.10, s32[4]{0:T(128)S(1)} %pad_add_fusion.place), custom_call_target="tpu_custom_call" | custom-call | tf_op jit(solution)/shard_map/pallas_call | solution.py:308
  (1 shorter events, 0.0 us)
Async XLA Ops:
  0.6 1.0 %copy-start = (f32[32,32,128]{2,1,0:T(8,128)S(1)}, f32[32,32,128]{2,1,0:T(8,128)}, u32[]{:S(2)}) copy-start(f32[32,32,128]{2,1,0:T(8,128)} %source.3) | copy-start | bytes 1572868
  1.7 1.0 %copy-start.1 = (f32[32,32,128]{2,1,0:T(8,128)S(1)}, f32[32,32,128]{2,1,0:T(8,128)}, u32[]{:S(2)}) copy-start(f32[32,32,128]{2,1,0:T(8,128)} %potential.3) | copy-start | bytes 1572868
  2.7 0.7 copy-start.2
  4.1 36.8 %collective-permute-start = (f32[129,8,128]{2,1,0:T(8,128)S(1)}, f32[129,8,128]{2,1,0:T(8,128)S(1)}, u32[]{:S(2)}, u32[]{:S(2)}) collective-permute-start(f32[129,8,128]{2,1,0:T(8,128)S(1)} %get-tuple-element.9), channel_id=1, source_target_pairs={{0,1},{1,2},{2,3},{3,4},{4,5},{5,6},{6,7},{7,8},{8,9},{9,10},{10,1... | collective-permute-start | bytes 1585160 | tf_op jit(solution)/shard_map/ppermute | solution.py:287
  8.1 32.8 %collective-permute-start.1 = (f32[129,8,128]{2,1,0:T(8,128)S(1)}, f32[129,8,128]{2,1,0:T(8,128)S(1)}, u32[]{:S(2)}, u32[]{:S(2)}) collective-permute-start(f32[129,8,128]{2,1,0:T(8,128)S(1)} %get-tuple-element.10), channel_id=1, source_target_pairs={{1,0},{2,1},{3,2},{4,3},{5,4},{6,5},{7,6},{8,7},{9,8},{10,9},{11,1... | collective-permute-start | bytes 1585160 | tf_op jit(solution)/shard_map/ppermute | solution.py:287
  43.0 25.1 %collective-permute-start.2 = (f32[65,32,128]{2,1,0:T(8,128)}, f32[65,32,128]{2,1,0:T(8,128)S(1)}, u32[]{:S(2)}, u32[]{:S(2)}) collective-permute-start(f32[65,32,128]{2,1,0:T(8,128)} %get-tuple-element.13), channel_id=1, source_target_pairs={{0,32},{32,64},{64,96},{96,128},{128,160},{160,192},{192,224},{224... | collective-permute-start | bytes 3194888 | tf_op jit(solution)/shard_map/ppermute | solution.py:287
  46.0 22.1 %collective-permute-start.3 = (f32[65,32,128]{2,1,0:T(8,128)}, f32[65,32,128]{2,1,0:T(8,128)}, u32[]{:S(2)}, u32[]{:S(2)}) collective-permute-start(f32[65,32,128]{2,1,0:T(8,128)} %get-tuple-element.14), channel_id=1, source_target_pairs={{32,0},{64,32},{96,64},{128,96},{160,128},{192,160},{224,192},{256... | collective-permute-start | bytes 3194888 | tf_op jit(solution)/shard_map/ppermute | solution.py:287
  47.9 20.2 %all-to-all-start.1 = ((f32[32,1,128]{2,1,0:T(1,128)}), f32[32,1,128]{2,1,0:T(1,128)S(1)}, u32[]{:S(2)}, u32[]{:S(2)}) async-start(f32[32,1,128]{2,1,0:T(1,128)} %bitcast.4), calls=%async_computation.1 | async-start | bytes 32768 | tf_op jit(solution)/shard_map/all_to_all | solution.py:302

commit v2 on v0

v2 whole, which is shorter than its diff:
```python
import jax
import jax.numpy as jnp
from jax import lax
from jax.experimental import pallas as pl
from jax.experimental.pallas import tpu as pltpu
from jax.sharding import PartitionSpec as P

GROUP = "group"
MEMBER = "member"
N = 32
NZ = 128
K = N // 2
H = 16
KH = H // 2
NX = N + 2 * H
NK = K + 2 * KH
NC = NX // 2
PAD = 8
SIXTH = 1.0 / 6.0
F32 = jnp.float32
MIB = 1024 * 1024
CHUNKS = 1
EXTRA, FLAGS = 4 * H, 4 * H + 1
SEGMENT = 4 * H + 2


def lanes(rows):
    return lax.broadcasted_iota(jnp.int32, (rows, NZ), 1)


def rows_of(rows):
    return lax.broadcasted_iota(jnp.int32, (rows, NZ), 0)


def split(ref, x, first):
    even = ref[x, pl.ds(0, K, stride=2), :]
    odd = ref[x, pl.ds(1, K, stride=2), :]
    return jnp.where(first, even, odd), jnp.where(first, odd, even)


def pack_kernel(source_any, potential_any, refined_any, up, down, part, own_flags, source, potential, refined, sems):
    size = N // CHUNKS
    flag_copy = pltpu.make_async_copy(refined_any, refined, sems.at[2 * CHUNKS])
    flag_copy.start()
    copies = []
    for c in range(CHUNKS):
        planes = pl.ds(c * size, size)
        pair = []
        for a, (src, dst) in enumerate(((source_any, source), (potential_any, potential))):
            pair.append(pltpu.make_async_copy(src.at[planes], dst.at[planes], sems.at[2 * c + a]))
        for copy in pair:
            copy.start()
        copies.append(pair)
    zp = lanes(K) % 2
    row = rows_of(KH)
    zp8 = lanes(KH) % 2
    acc = [jnp.zeros((K, NZ), F32), jnp.zeros((K, NZ), F32)]
    for x in range(N):
        if x % size == 0:
            for copy in copies[x // size]:
                copy.wait()
        j = x % 2
        first = zp == j
        pr, pb = split(potential, x, first)
        sr, sb = split(source, x, first)
        acc[j] = acc[j] + (sr + sb)
        up[x] = pr[KH:]
        down[x] = pr[:KH]
        up[N + x] = pb[KH:]
        down[N + x] = pb[:KH]
        beyond_up = jnp.where((row == 0) & (zp8 == j), pltpu.roll(pb[:KH], 1, 0), 0.0)
        beyond_down = jnp.where((row == KH - 1) & (zp8 != j), pltpu.roll(pb[KH:], KH - 1, 0), 0.0)
        up[2 * N + x] = sr[KH:] + beyond_up
        down[2 * N + x] = sr[:KH] + beyond_down
        up[3 * N + x] = sb[KH:]
        down[3 * N + x] = sb[:KH]
    total = jnp.sum(acc[0] + acc[1], axis=0, keepdims=True)
    part[...] = jnp.broadcast_to(total, part.shape)
    flag_copy.wait()
    box = lanes(KH) // N
    flags = jnp.zeros((KH, NZ), F32)
    for b in range(NZ // N):
        on = jnp.where(refined[0, 0, b] == 1, 1.0, 0.0).astype(F32)
        flags = jnp.where(box == b, on, flags)
    for ref in (up, down):
        ref[4 * N] = flags
    own_flags[...] = flags


def middle_kernel(source, potential, flags, low, high, parts, first_half, second_half, part, own, sem):
    copy = pltpu.make_async_copy(flags, own, sem)
    copy.start()
    zp = lanes(K) % 2
    for x in range(N):
        ref, at = (first_half, x) if x < H else (second_half, x - H)
        here = zp == x % 2
        fields = split(potential, x, here) + split(source, x, here)
        for a in range(4):
            ref[a * H + at, :KH] = low[a * N + x]
            ref[a * H + at, KH : KH + K] = fields[a]
            ref[a * H + at, KH + K :] = high[a * N + x]
            if a == 1 and x in (H - 1, H):
                far = second_half if x == H - 1 else first_half
                far[EXTRA, :KH] = low[a * N + x]
                far[EXTRA, KH : KH + K] = fields[a]
                far[EXTRA, KH + K :] = high[a * N + x]
    copy.wait()
    for ref in (first_half, second_half):
        ref[FLAGS, :KH] = low[4 * N]
        ref[FLAGS, KH : 2 * KH] = own[...]
        ref[FLAGS, 2 * KH : 3 * KH] = own[...]
        ref[FLAGS, 3 * KH :] = high[4 * N]
    part[...] = jnp.broadcast_to(jnp.sum(parts[...], axis=0, keepdims=True), part.shape)


def lane_sum(values, step, z):
    left = jnp.where(z < step, 0.0, pltpu.roll(values, step, 1))
    right = jnp.where(z >= NZ - step, 0.0, pltpu.roll(values, NZ - step, 1))
    return left + right


def cycle_kernel(seg0, seg1, seg2, seg3, parts, place, smoothed, residual, red, black, coarse, corr):
    segments = (seg0, seg1, seg2, seg3)
    cells = place[2] * place[3] * (N * N * NZ)
    mean = jnp.sum(parts[...]) / cells.astype(F32)

    def field(a, x, rows=slice(None)):
        return segments[x // H][a * H + x % H, rows, :]

    def right_side(colour, x, rows=slice(None)):
        return field(2 + colour, x, rows) - mean

    def sides(ref, x, r0, rows, colour, zp):
        below = ref[x, r0 - 1 : r0 - 1 + rows, :]
        above = ref[x, r0 + 1 : r0 + 1 + rows, :]
        return jnp.where(zp == (x + colour) % 2, below, above)

    def neighbours(ref, x, r0, rows, colour, z):
        centre = ref[x, r0 : r0 + rows, :]
        along_x = ref[x - 1, r0 : r0 + rows, :] + ref[x + 1, r0 : r0 + rows, :]
        return along_x + (centre + sides(ref, x, r0, rows, colour, z % 2)) + lane_sum(centre, 1, z)

    z = lanes(NK)
    zp = z % 2
    row = rows_of(NK)
    whole = slice(PAD, PAD + NK)
    for x in range(NX):
        centre = field(1, x)
        before = field(1, x - 1) if x > 0 else seg0[EXTRA]
        after = field(1, x + 1) if x < NX - 1 else seg3[EXTRA]
        below = jnp.where(row == 0, 0.0, pltpu.roll(centre, 1, 0))
        above = jnp.where(row == NK - 1, 0.0, pltpu.roll(centre, NK - 1, 0))
        side = jnp.where(zp == x % 2, below, above)
        total = (before + after) + (centre + side) + lane_sum(centre, 1, z)
        on = segments[x // H][FLAGS] > 0.5
        red[x, whole, :] = jnp.where(on, (right_side(0, x) + total) * SIXTH, field(0, x))
    for step in range(1, 4):
        colour = step % 2
        dst, src = (red, black) if colour == 0 else (black, red)
        if step == 1:
            for x in (0, NX - 1):
                black[x, whole, :] = field(1, x)
        for x in range(step, NX - step):
            on = segments[x // H][FLAGS] > 0.5
            old = field(1, x) if step == 1 else dst[x, whole, :]
            total = neighbours(src, x, PAD, NK, colour, z)
            dst[x, whole, :] = jnp.where(on, (right_side(colour, x) + total) * SIXTH, old)

    for cx in range(2, NC - 2):
        x = 2 * cx
        u = [red[x + d, whole, :] + black[x + d, whole, :] for d in (-1, 0, 1, 2)]
        w = u[1] + u[2]
        s = (field(2, x) + field(3, x)) + (field(2, x + 1) + field(3, x + 1)) - 4.0 * mean
        total = s - 4.0 * w + (u[0] + u[3]) + lane_sum(w, 1, z)
        for j in range(2):
            total = total + sides(black, x + j, PAD, NK, 0, zp) + sides(red, x + j, PAD, NK, 1, zp)
        coarse[cx] = total * 0.5

    global_row = place[1] * K + row - KH
    row_gain = jnp.where((global_row >= 0) & (global_row < place[3] * K), SIXTH, 0.0).astype(F32)
    parity = (row + z // 2) % 2

    def gain_at(cx):
        if KH <= cx < KH + N // 2:
            return row_gain
        at = place[0] * K + cx - KH
        return row_gain * jnp.where((at >= 0) & (at < place[2] * K), 1.0, 0.0).astype(F32)

    for cx in range(2, NC - 2):
        total = coarse[cx]
        pair = jnp.where(zp == 0, pltpu.roll(total, NZ - 1, 1), pltpu.roll(total, 1, 1))
        total = total + pair
        coarse[cx] = total
        corr[cx, whole, :] = jnp.where(parity == cx % 2, total * gain_at(cx), 0.0)
    for step in range(1, 4):
        for cx in range(2 + step, NC - 2 - step):
            centre = corr[cx, whole, :]
            along_y = corr[cx, PAD - 1 : PAD - 1 + NK, :] + corr[cx, PAD + 1 : PAD + 1 + NK, :]
            along_x = corr[cx - 1, whole, :] + corr[cx + 1, whole, :]
            update = (coarse[cx] + (along_x + along_y) + lane_sum(centre, 2, z)) * gain_at(cx)
            corr[cx, whole, :] = jnp.where(parity == (step + cx) % 2, update, centre)

    rows = slice(PAD + 4, PAD + NK - 4)
    for cx in range(5, NC - 5):
        add = corr[cx, rows, :]
        for ref in (red, black):
            for x in (2 * cx, 2 * cx + 1):
                ref[x, rows, :] = ref[x, rows, :] + add

    z2 = lanes(NK - 8)
    for step in range(4):
        colour = step % 2
        dst, src = (red, black) if colour == 0 else (black, red)
        for x in range(12 + step, NX - 12 - step):
            on = segments[x // H][FLAGS, 4 : NK - 4, :] > 0.5
            total = neighbours(src, x, PAD + 4, NK - 8, colour, z2)
            update = (right_side(colour, x, slice(4, NK - 4)) + total) * SIXTH
            dst[x, rows, :] = jnp.where(on, update, dst[x, rows, :])

    zk = lanes(K)
    r0 = PAD + KH
    own = slice(KH, KH + K)
    for x in range(H, H + N):
        here = zk % 2 == x % 2
        r = red[x, r0 : r0 + K, :]
        b = black[x, r0 : r0 + K, :]
        res_r = right_side(0, x, own) - 6.0 * r + neighbours(black, x, r0, K, 0, zk)
        res_b = right_side(1, x, own) - 6.0 * b + neighbours(red, x, r0, K, 1, zk)
        for ref, one, two in ((smoothed, r, b), (residual, res_r, res_b)):
            ref[x - H, pl.ds(0, K, stride=2), :] = jnp.where(here, one, two)
            ref[x - H, pl.ds(1, K, stride=2), :] = jnp.where(here, two, one)


def shape(*dims):
    return jax.ShapeDtypeStruct(dims, F32)


VMEM = pl.BlockSpec(memory_space=pltpu.VMEM)
SMEM = pl.BlockSpec(memory_space=pltpu.SMEM)
ANY = pl.BlockSpec(memory_space=pltpu.HBM)


def call(kernel, ins, outs, mib, bytes_moved, scratch=()):
    return pl.pallas_call(
        kernel,
        out_shape=outs,
        in_specs=ins,
        out_specs=[VMEM] * len(outs),
        scratch_shapes=list(scratch),
        cost_estimate=pl.CostEstimate(flops=0, bytes_accessed=bytes_moved * MIB, transcendentals=0),
        compiler_params=pltpu.CompilerParams(vmem_limit_bytes=mib * MIB),
    )


def build_pack(groups):
    side = shape(4 * N + 1, KH, NZ)
    return call(
        pack_kernel,
        [ANY, ANY, ANY],
        [side, side, shape(groups, NZ), shape(KH, NZ)],
        56,
        4,
        [
            pltpu.VMEM((N, N, NZ), F32),
            pltpu.VMEM((N, N, NZ), F32),
            pltpu.SMEM((1, 1, NZ // N), jnp.int32),
            pltpu.SemaphoreType.DMA((2 * CHUNKS + 1,)),
        ],
    )


def build_middle(members):
    half = shape(SEGMENT, NK, NZ)
    return call(
        middle_kernel,
        [VMEM, VMEM, ANY, VMEM, VMEM, VMEM],
        [half, half, shape(members, NZ)],
        8,
        6,
        [pltpu.VMEM((KH, NZ), F32), pltpu.SemaphoreType.DMA],
    )


def build_cycle():
    padded = pltpu.VMEM((NX, NK + 2 * PAD, NZ), F32)
    return call(
        cycle_kernel,
        [VMEM] * 5 + [SMEM],
        [shape(N, N, NZ), shape(N, N, NZ)],
        16,
        20,
        [padded, padded, pltpu.VMEM((NC, NK, NZ), F32), pltpu.VMEM((NC, NK + 2 * PAD, NZ), F32)],
    )


def per_device(source, potential, refined):
    groups, members = lax.axis_size(GROUP), lax.axis_size(MEMBER)

    def both_ways(up, down, axis):
        size = lax.axis_size(axis)
        pairs = [(i, i + 1) for i in range(size - 1)]
        return lax.ppermute(up, axis, pairs), lax.ppermute(down, axis, [(b, a) for a, b in pairs])

    up, down, part, flags = build_pack(groups)(source, potential, refined)
    low, high = both_ways(up, down, MEMBER)
    parts = lax.all_to_all(part, GROUP, 0, 0, tiled=True)
    first_half, second_half, part = build_middle(members)(source, potential, flags, low, high, parts)
    before, after = both_ways(second_half, first_half, GROUP)
    parts = lax.all_to_all(part, MEMBER, 0, 0, tiled=True)
    place = jnp.stack(
        [lax.axis_index(GROUP), lax.axis_index(MEMBER), jnp.int32(groups), jnp.int32(members)]
    ).astype(jnp.int32)
    return build_cycle()(before, first_half, second_half, after, parts, place)


def solution(mesh):
    spec = P(GROUP, MEMBER, None)
    return jax.shard_map(
        per_device, mesh=mesh, in_specs=(spec, spec, spec), out_specs=(spec, spec), check_vma=False
    )
```

time: 292 us -> 73.8 us (0.25)
  the two profiles are of different devices: /device:TPU:223 before, /device:TPU:1 now
where the time goes in v2:
time: 73.8 us; the launch traced here: 73.4 us
  blocking collectives  31.6 us (43%)
  starting transfers between devices  21.8 us (30%)
  Pallas kernels  10.1 us (14%)
  waiting for transfers between devices  8.43 us (11%)
  between operations  0.74 us (1%)
    all_to_all x1, blocking collectives, per_device(): parts = lax.all_to_all(part, GROUP, 0, 0, tiled=True)  31.6 us
    all_to_all x1, starting transfers between devices, per_device(): parts = lax.all_to_all(part, MEMBER, 0, 0, tiled=True)  11.7 us
    all_to_all x1, waiting for transfers between devices, per_device(): parts = lax.all_to_all(part, MEMBER, 0, 0, tiled=True)  8.42 us
    ppermute x2, starting transfers between devices, both_ways(): lax.ppermute(up, axis, pairs)  6.97 us
    pallas_call x1, Pallas kernels, per_device(): return build_cycle()(before, first_half, second_half, after, parts, place)  6.83 us
    ppermute x2, starting transfers between devices, both_ways(): lax.ppermute(down, axis, [(b, a) for a, b in pairs])  3.21 us
    pallas_call x1, Pallas kernels, per_device(): up, down, part, flags = build_pack(groups)(source, potential, refined)  2.42 us
  transfers between devices with their start and end apart: 5, of which 1 were waited for; matrix products, arithmetic and copies ran while one was open for 0% of the time, Pallas kernels for 0%

profile of v2, /device:TPU:1, one launch (start us, length us, event | category | flops | bytes accessed | tf_op | source)
XLA Modules:
  0.0 73.4 jit_solution(15082931043449743417)
XLA Ops:
  0.6 0.0 copy-start.1
  0.6 0.0 copy-start
  0.6 2.4 %shard_map.50 = (f32[129,8,128]{2,1,0:T(8,128)}, f32[129,8,128]{2,1,0:T(8,128)}, f32[32,128]{1,0:T(8,128)}, f32[8,128]{1,0:T(8,128)}) custom-call(f32[32,32,128]{2,1,0:T(8,128)} %source.1, f32[32,32,128]{2,1,0:T(8,128)} %potential.1, s32[1,1,4]{2,1,0:T(1,128)} %refined_any.1), custom_call_target="tpu_custom_call" | custom-call | bytes 4194304 | tf_op jit(solution)/shard_map/pallas_call | solution.py:304
  3.1 4.0 %collective-permute-start = (f32[129,8,128]{2,1,0:T(8,128)}, f32[129,8,128]{2,1,0:T(8,128)S(1)}, u32[]{:S(2)}, u32[]{:S(2)}) collective-permute-start(f32[129,8,128]{2,1,0:T(8,128)} %get-tuple-element.10), channel_id=1, source_target_pairs={{0,1},{1,2},{2,3},{3,4},{4,5},{5,6},{6,7},{7,8},{8,9},{9,10},{10,1... | collective-permute-start | bytes 1585160 | tf_op jit(solution)/shard_map/ppermute | solution.py:302
  7.1 1.3 %collective-permute-start.1 = (f32[129,8,128]{2,1,0:T(8,128)}, f32[129,8,128]{2,1,0:T(8,128)S(1)}, u32[]{:S(2)}, u32[]{:S(2)}) collective-permute-start(f32[129,8,128]{2,1,0:T(8,128)} %get-tuple-element.11), channel_id=1, source_target_pairs={{1,0},{2,1},{3,2},{4,3},{5,4},{6,5},{7,6},{8,7},{9,8},{10,9},{11,1... | collective-permute-start | bytes 1585160 | tf_op jit(solution)/shard_map/ppermute | solution.py:302
  8.4 31.6 %all_to_all.22 = f32[32,1,128]{2,1,0:T(1,128)S(1)} all-to-all(f32[32,1,128]{2,1,0:T(1,128)} %bitcast.12), channel_id=1, replica_groups=mesh['group'=32,'member'=32] {'group'}, dimensions={0} | all-to-all | bytes 32768 | tf_op jit(solution)/shard_map/all_to_all | solution.py:306
  40.0 0.0 collective-permute-done.low
  40.0 0.0 collective-permute-done.1.high
  40.0 0.0 copy-done.1
  40.0 0.0 copy-done
  40.0 0.0 copy-start.2
  40.0 0.7 copy-done.2
  40.7 0.8 %shard_map.51 = (f32[66,32,128]{2,1,0:T(8,128)S(1)}, f32[66,32,128]{2,1,0:T(8,128)S(1)}, f32[32,128]{1,0:T(8,128)}) custom-call(f32[32,32,128]{2,1,0:T(8,128)S(1)} %copy-done, f32[32,32,128]{2,1,0:T(8,128)S(1)} %copy-done.1, f32[8,128]{1,0:T(8,128)S(1)} %copy-done.2, f32[129,8,128]{2,1,0:T(8,128)S(1)} %collective-permute-done.low, ...), custom_call_target="tpu_custom_call" | custom-call | bytes 6291456 | tf_op jit(solution)/shard_map/pallas_call | solution.py:307
  41.5 3.0 %collective-permute-start.2 = (f32[66,32,128]{2,1,0:T(8,128)S(1)}, f32[66,32,128]{2,1,0:T(8,128)S(1)}, u32[]{:S(2)}, u32[]{:S(2)}) collective-permute-start(f32[66,32,128]{2,1,0:T(8,128)S(1)} %get-tuple-element.13.seg2), channel_id=1, source_target_pairs={{0,32},{32,64},{64,96},{96,128},{128,160},{160,192},{192,224},{224... | collective-permute-start | bytes 3244040 | tf_op jit(solution)/shard_map/ppermute | solution.py:302
  44.5 1.9 %collective-permute-start.3 = (f32[66,32,128]{2,1,0:T(8,128)S(1)}, f32[66,32,128]{2,1,0:T(8,128)}, u32[]{:S(2)}, u32[]{:S(2)}) collective-permute-start(f32[66,32,128]{2,1,0:T(8,128)S(1)} %get-tuple-element.14.seg1), channel_id=1, source_target_pairs={{32,0},{64,32},{96,64},{128,96},{160,128},{192,160},{224,192},{256... | collective-permute-start | bytes 3244040 | tf_op jit(solution)/shard_map/ppermute | solution.py:302
  46.4 11.7 %all-to-all-start.1 = ((f32[32,1,128]{2,1,0:T(1,128)}), f32[32,1,128]{2,1,0:T(1,128)S(1)}, u32[]{:S(2)}, u32[]{:S(2)}) async-start(f32[32,1,128]{2,1,0:T(1,128)} %bitcast.4), calls=%async_computation.1 | async-start | bytes 32768 | tf_op jit(solution)/shard_map/all_to_all | solution.py:309
  58.1 0.1 pad_add_fusion.place
  58.2 8.4 %all-to-all-done.1 = f32[32,1,128]{2,1,0:T(1,128)S(1)} async-done(((f32[32,1,128]{2,1,0:T(1,128)}), f32[32,1,128]{2,1,0:T(1,128)S(1)}, u32[]{:S(2)}, u32[]{:S(2)}) %all-to-all-start.1) | async-done | bytes 16416 | tf_op jit(solution)/shard_map/all_to_all | solution.py:309
  66.6 0.0 collective-permute-done.2.seg0
  66.6 0.0 collective-permute-done.3.seg3
  66.6 6.8 %shard_map.52 = (f32[32,32,128]{2,1,0:T(8,128)}, f32[32,32,128]{2,1,0:T(8,128)}) custom-call(f32[66,32,128]{2,1,0:T(8,128)S(1)} %collective-permute-done.2.seg0, f32[66,32,128]{2,1,0:T(8,128)S(1)} %get-tuple-element.14.seg1, f32[66,32,128]{2,1,0:T(8,128)S(1)} %get-tuple-element.13.seg2, f32[66,32,128]{2,1,0:T(8,128)} %collective-permute-done.3.seg3, ...), custom_call_target="tpu_custom_call" | custom-call | bytes 20971520 | tf_op jit(solution)/shard_map/pallas_call | solution.py:313
  (1 shorter events, 0.0 us)
Async XLA Ops:
  0.6 39.3 %copy-start.1 = (f32[32,32,128]{2,1,0:T(8,128)S(1)}, f32[32,32,128]{2,1,0:T(8,128)}, u32[]{:S(2)}) copy-start(f32[32,32,128]{2,1,0:T(8,128)} %potential.1) | copy-start | bytes 1572868
  0.6 39.3 %copy-start = (f32[32,32,128]{2,1,0:T(8,128)S(1)}, f32[32,32,128]{2,1,0:T(8,128)}, u32[]{:S(2)}) copy-start(f32[32,32,128]{2,1,0:T(8,128)} %source.1) | copy-start | bytes 1572868
  3.1 36.9 %collective-permute-start = (f32[129,8,128]{2,1,0:T(8,128)}, f32[129,8,128]{2,1,0:T(8,128)S(1)}, u32[]{:S(2)}, u32[]{:S(2)}) collective-permute-start(f32[129,8,128]{2,1,0:T(8,128)} %get-tuple-element.10), channel_id=1, source_target_pairs={{0,1},{1,2},{2,3},{3,4},{4,5},{5,6},{6,7},{7,8},{8,9},{9,10},{10,1... | collective-permute-start | bytes 1585160 | tf_op jit(solution)/shard_map/ppermute | solution.py:302
  7.1 32.9 %collective-permute-start.1 = (f32[129,8,128]{2,1,0:T(8,128)}, f32[129,8,128]{2,1,0:T(8,128)S(1)}, u32[]{:S(2)}, u32[]{:S(2)}) collective-permute-start(f32[129,8,128]{2,1,0:T(8,128)} %get-tuple-element.11), channel_id=1, source_target_pairs={{1,0},{2,1},{3,2},{4,3},{5,4},{6,5},{7,6},{8,7},{9,8},{10,9},{11,1... | collective-permute-start | bytes 1585160 | tf_op jit(solution)/shard_map/ppermute | solution.py:302
  40.0 0.7 copy-start.2
  41.5 25.1 %collective-permute-start.2 = (f32[66,32,128]{2,1,0:T(8,128)S(1)}, f32[66,32,128]{2,1,0:T(8,128)S(1)}, u32[]{:S(2)}, u32[]{:S(2)}) collective-permute-start(f32[66,32,128]{2,1,0:T(8,128)S(1)} %get-tuple-element.13.seg2), channel_id=1, source_target_pairs={{0,32},{32,64},{64,96},{96,128},{128,160},{160,192},{192,224},{224... | collective-permute-start | bytes 3244040 | tf_op jit(solution)/shard_map/ppermute | solution.py:302
  44.5 22.1 %collective-permute-start.3 = (f32[66,32,128]{2,1,0:T(8,128)S(1)}, f32[66,32,128]{2,1,0:T(8,128)}, u32[]{:S(2)}, u32[]{:S(2)}) collective-permute-start(f32[66,32,128]{2,1,0:T(8,128)S(1)} %get-tuple-element.14.seg1), channel_id=1, source_target_pairs={{32,0},{64,32},{96,64},{128,96},{160,128},{192,160},{224,192},{256... | collective-permute-start | bytes 3244040 | tf_op jit(solution)/shard_map/ppermute | solution.py:302
  46.4 20.2 %all-to-all-start.1 = ((f32[32,1,128]{2,1,0:T(1,128)}), f32[32,1,128]{2,1,0:T(1,128)S(1)}, u32[]{:S(2)}, u32[]{:S(2)}) async-start(f32[32,1,128]{2,1,0:T(1,128)} %bitcast.4), calls=%async_computation.1 | async-start | bytes 32768 | tf_op jit(solution)/shard_map/all_to_all | solution.py:309

commit v3 on v2

--- a/solution.py
+++ b/solution.py
@@ -1,3 +1,5 @@
+import functools
+
 import jax
 import jax.numpy as jnp
 from jax import lax
@@ -38,7 +40,7 @@
     return jnp.where(first, even, odd), jnp.where(first, odd, even)
 
 
-def pack_kernel(source_any, potential_any, refined_any, up, down, part, own_flags, source, potential, refined, sems):
+def pack_kernel(source_any, potential_any, refined_any, up, down, part, source, potential, refined, sems):
     size = N // CHUNKS
     flag_copy = pltpu.make_async_copy(refined_any, refined, sems.at[2 * CHUNKS])
     flag_copy.start()
@@ -75,7 +77,6 @@
         up[3 * N + x] = sb[KH:]
         down[3 * N + x] = sb[:KH]
     total = jnp.sum(acc[0] + acc[1], axis=0, keepdims=True)
-    part[...] = jnp.broadcast_to(total, part.shape)
     flag_copy.wait()
     box = lanes(KH) // N
     flags = jnp.zeros((KH, NZ), F32)
@@ -84,12 +85,15 @@
         flags = jnp.where(box == b, on, flags)
     for ref in (up, down):
         ref[4 * N] = flags
-    own_flags[...] = flags
-
-
-def middle_kernel(source, potential, flags, low, high, parts, first_half, second_half, part, own, sem):
-    copy = pltpu.make_async_copy(flags, own, sem)
-    copy.start()
+    part[...] = jnp.where(rows_of(part.shape[0]) % 2 == 0, total, flags[:1])
+
+
+def middle_kernel(source, potential, low, high, parts, first_half, second_half, part):
+    row = rows_of(parts.shape[0])
+    mine = jnp.where(row == 2 * lax.axis_index(GROUP) + 1, parts[...], 0.0)
+    own = jnp.broadcast_to(jnp.sum(mine, axis=0, keepdims=True), (KH, NZ))
+    totals = jnp.where(row % 2 == 0, parts[...], 0.0)
+    part[...] = jnp.broadcast_to(jnp.sum(totals, axis=0, keepdims=True), part.shape)
     zp = lanes(K) % 2
     for x in range(N):
         ref, at = (first_half, x) if x < H else (second_half, x - H)
@@ -104,13 +108,11 @@
                 far[EXTRA, :KH] = low[a * N + x]
                 far[EXTRA, KH : KH + K] = fields[a]
                 far[EXTRA, KH + K :] = high[a * N + x]
-    copy.wait()
     for ref in (first_half, second_half):
         ref[FLAGS, :KH] = low[4 * N]
-        ref[FLAGS, KH : 2 * KH] = own[...]
-        ref[FLAGS, 2 * KH : 3 * KH] = own[...]
+        ref[FLAGS, KH : 2 * KH] = own
+        ref[FLAGS, 2 * KH : 3 * KH] = own
         ref[FLAGS, 3 * KH :] = high[4 * N]
-    part[...] = jnp.broadcast_to(jnp.sum(parts[...], axis=0, keepdims=True), part.shape)
 
 
 def lane_sum(values, step, z):
@@ -119,10 +121,14 @@
     return left + right
 
 
-def cycle_kernel(seg0, seg1, seg2, seg3, parts, place, smoothed, residual, red, black, coarse, corr):
+def cycle_kernel(
+    cells, seg0, seg1, seg2, seg3_any, parts, place, smoothed, residual, red, black, coarse, corr, seg3, sem
+):
+    load = pltpu.make_async_copy(seg3_any, seg3, sem)
+    load.start()
     segments = (seg0, seg1, seg2, seg3)
-    cells = place[2] * place[3] * (N * N * NZ)
-    mean = jnp.sum(parts[...]) / cells.astype(F32)
+    total = jnp.sum(jnp.sum(parts[...], axis=0, keepdims=True), axis=1, keepdims=True)
+    mean = total * (1.0 / cells)
 
     def field(a, x, rows=slice(None)):
         return segments[x // H][a * H + x % H, rows, :]
@@ -145,6 +151,8 @@
     row = rows_of(NK)
     whole = slice(PAD, PAD + NK)
     for x in range(NX):
+        if x + 1 == 3 * H:
+            load.wait()
         centre = field(1, x)
         before = field(1, x - 1) if x > 0 else seg0[EXTRA]
         after = field(1, x + 1) if x < NX - 1 else seg3[EXTRA]
@@ -257,7 +265,7 @@
     return call(
         pack_kernel,
         [ANY, ANY, ANY],
-        [side, side, shape(groups, NZ), shape(KH, NZ)],
+        [side, side, shape(2 * groups, NZ)],
         56,
         4,
         [
@@ -273,23 +281,29 @@
     half = shape(SEGMENT, NK, NZ)
     return call(
         middle_kernel,
-        [VMEM, VMEM, ANY, VMEM, VMEM, VMEM],
+        [VMEM] * 5,
         [half, half, shape(members, NZ)],
         8,
         6,
-        [pltpu.VMEM((KH, NZ), F32), pltpu.SemaphoreType.DMA],
-    )
-
-
-def build_cycle():
+    )
+
+
+def build_cycle(cells):
     padded = pltpu.VMEM((NX, NK + 2 * PAD, NZ), F32)
     return call(
-        cycle_kernel,
-        [VMEM] * 5 + [SMEM],
+        functools.partial(cycle_kernel, cells),
+        [VMEM, VMEM, VMEM, ANY, VMEM, SMEM],
         [shape(N, N, NZ), shape(N, N, NZ)],
-        16,
+        9,
         20,
-        [padded, padded, pltpu.VMEM((NC, NK, NZ), F32), pltpu.VMEM((NC, NK + 2 * PAD, NZ), F32)],
+        [
+            padded,
+            padded,
+            pltpu.VMEM((NC, NK, NZ), F32),
+            pltpu.VMEM((NC, NK + 2 * PAD, NZ), F32),
+            pltpu.VMEM((SEGMENT, NK, NZ), F32),
+            pltpu.SemaphoreType.DMA,
+        ],
     )
 
 
@@ -301,16 +315,16 @@
         pairs = [(i, i + 1) for i in range(size - 1)]
         return lax.ppermute(up, axis, pairs), lax.ppermute(down, axis, [(b, a) for a, b in pairs])
 
-    up, down, part, flags = build_pack(groups)(source, potential, refined)
+    up, down, part = build_pack(groups)(source, potential, refined)
     low, high = both_ways(up, down, MEMBER)
     parts = lax.all_to_all(part, GROUP, 0, 0, tiled=True)
-    first_half, second_half, part = build_middle(members)(source, potential, flags, low, high, parts)
+    first_half, second_half, part = build_middle(members)(source, potential, low, high, parts)
     before, after = both_ways(second_half, first_half, GROUP)
     parts = lax.all_to_all(part, MEMBER, 0, 0, tiled=True)
     place = jnp.stack(
         [lax.axis_index(GROUP), lax.axis_index(MEMBER), jnp.int32(groups), jnp.int32(members)]
     ).astype(jnp.int32)
-    return build_cycle()(before, first_half, second_half, after, parts, place)
+    return build_cycle(groups * members * N * N * NZ)(before, first_half, second_half, after, parts, place)
 
 
 def solution(mesh):

time: 73.8 us -> 73.6 us (level)
  no operation moved by 1% of the time
where the time goes in v3:
time: 73.6 us; the launch traced here: 73.3 us
  blocking collectives  32 us (43%)
  starting transfers between devices  22 us (30%)
  Pallas kernels  10 us (14%)
  waiting for transfers between devices  8.43 us (11%)
    all_to_all x1, blocking collectives, per_device(): parts = lax.all_to_all(part, GROUP, 0, 0, tiled=True)  32 us
    all_to_all x1, starting transfers between devices, per_device(): parts = lax.all_to_all(part, MEMBER, 0, 0, tiled=True)  11.7 us
    all_to_all x1, waiting for transfers between devices, per_device(): parts = lax.all_to_all(part, MEMBER, 0, 0, tiled=True)  8.42 us
    ppermute x2, starting transfers between devices, both_ways(): lax.ppermute(up, axis, pairs)  7.17 us
    pallas_call x1, Pallas kernels, per_device(): build_cycle(groups * members * N * N * NZ)  6.83 us
    ppermute x2, starting transfers between devices, both_ways(): lax.ppermute(down, axis, [(b, a) for a, b in pairs])  3.21 us
    pallas_call x1, Pallas kernels, per_device(): up, down, part = build_pack(groups)(source, potential, refined)  2.39 us
  transfers between devices with their start and end apart: 5, of which 1 were waited for; matrix products, arithmetic and copies ran while one was open for 0% of the time, Pallas kernels for 0%

profile of v3, /device:TPU:1, one launch (start us, length us, event | category | flops | bytes accessed | tf_op | source)
XLA Modules:
  0.0 73.3 jit_solution(4821779153989983222)
XLA Ops:
  0.6 0.0 copy-start.1
  0.6 0.0 copy-start
  0.6 2.4 %shard_map.50 = (f32[129,8,128]{2,1,0:T(8,128)}, f32[129,8,128]{2,1,0:T(8,128)}, f32[64,128]{1,0:T(8,128)}) custom-call(f32[32,32,128]{2,1,0:T(8,128)} %source.1, f32[32,32,128]{2,1,0:T(8,128)} %potential.1, s32[1,1,4]{2,1,0:T(1,128)} %refined_any.1), custom_call_target="tpu_custom_call" | custom-call | bytes 4194304 | tf_op jit(solution)/shard_map/pallas_call | solution.py:318
  3.1 4.0 %collective-permute-start = (f32[129,8,128]{2,1,0:T(8,128)}, f32[129,8,128]{2,1,0:T(8,128)S(1)}, u32[]{:S(2)}, u32[]{:S(2)}) collective-permute-start(f32[129,8,128]{2,1,0:T(8,128)} %get-tuple-element.8), channel_id=1, source_target_pairs={{0,1},{1,2},{2,3},{3,4},{4,5},{5,6},{6,7},{7,8},{8,9},{9,10},{10,1... | collective-permute-start | bytes 1585160 | tf_op jit(solution)/shard_map/ppermute | solution.py:316
  7.0 1.3 %collective-permute-start.1 = (f32[129,8,128]{2,1,0:T(8,128)}, f32[129,8,128]{2,1,0:T(8,128)S(1)}, u32[]{:S(2)}, u32[]{:S(2)}) collective-permute-start(f32[129,8,128]{2,1,0:T(8,128)} %get-tuple-element.9), channel_id=1, source_target_pairs={{1,0},{2,1},{3,2},{4,3},{5,4},{6,5},{7,6},{8,7},{9,8},{10,9},{11,1... | collective-permute-start | bytes 1585160 | tf_op jit(solution)/shard_map/ppermute | solution.py:316
  8.3 32.0 %all_to_all.22 = f32[32,2,128]{2,1,0:T(2,128)S(1)} all-to-all(f32[32,2,128]{2,1,0:T(2,128)} %bitcast.10), channel_id=1, replica_groups=mesh['group'=32,'member'=32] {'group'}, dimensions={0} | all-to-all | bytes 65536 | tf_op jit(solution)/shard_map/all_to_all | solution.py:320
  40.3 0.0 collective-permute-done.low
  40.3 0.0 collective-permute-done.1.high
  40.3 0.0 copy-done.1
  40.3 0.0 copy-done
  40.4 0.8 %shard_map.51 = (f32[66,32,128]{2,1,0:T(8,128)S(1)}, f32[66,32,128]{2,1,0:T(8,128)S(1)}, f32[32,128]{1,0:T(8,128)}) custom-call(f32[32,32,128]{2,1,0:T(8,128)S(1)} %copy-done, f32[32,32,128]{2,1,0:T(8,128)S(1)} %copy-done.1, f32[129,8,128]{2,1,0:T(8,128)S(1)} %collective-permute-done.low, f32[129,8,128]{2,1,0:T(8,128)S(1)} %collective-permute-done.1.high, ...), custom_call_target="tpu_custom_call" | custom-call | bytes 6291456 | tf_op jit(solution)/shard_map/pallas_call | solution.py:321
  41.1 3.2 %collective-permute-start.2 = (f32[66,32,128]{2,1,0:T(8,128)S(1)}, f32[66,32,128]{2,1,0:T(8,128)S(1)}, u32[]{:S(2)}, u32[]{:S(2)}) collective-permute-start(f32[66,32,128]{2,1,0:T(8,128)S(1)} %get-tuple-element.11.seg2), channel_id=1, source_target_pairs={{0,32},{32,64},{64,96},{96,128},{128,160},{160,192},{192,224},{224... | collective-permute-start | bytes 3244040 | tf_op jit(solution)/shard_map/ppermute | solution.py:316
  44.3 1.9 %collective-permute-start.3 = (f32[66,32,128]{2,1,0:T(8,128)S(1)}, f32[66,32,128]{2,1,0:T(8,128)}, u32[]{:S(2)}, u32[]{:S(2)}) collective-permute-start(f32[66,32,128]{2,1,0:T(8,128)S(1)} %get-tuple-element.12.seg1), channel_id=1, source_target_pairs={{32,0},{64,32},{96,64},{128,96},{160,128},{192,160},{224,192},{256... | collective-permute-start | bytes 3244040 | tf_op jit(solution)/shard_map/ppermute | solution.py:316
  46.3 11.7 %all-to-all-start.1 = ((f32[32,1,128]{2,1,0:T(1,128)}), f32[32,1,128]{2,1,0:T(1,128)S(1)}, u32[]{:S(2)}, u32[]{:S(2)}) async-start(f32[32,1,128]{2,1,0:T(1,128)} %bitcast.3), calls=%async_computation.1 | async-start | bytes 32768 | tf_op jit(solution)/shard_map/all_to_all | solution.py:323
  58.0 0.1 pad_add_fusion.place
  58.0 8.4 %all-to-all-done.1 = f32[32,1,128]{2,1,0:T(1,128)S(1)} async-done(((f32[32,1,128]{2,1,0:T(1,128)}), f32[32,1,128]{2,1,0:T(1,128)S(1)}, u32[]{:S(2)}, u32[]{:S(2)}) %all-to-all-start.1) | async-done | bytes 16416 | tf_op jit(solution)/shard_map/all_to_all | solution.py:323
  66.5 0.0 collective-permute-done.2.seg0
  66.5 0.0 collective-permute-done.3.seg3_any
  66.5 6.8 %shard_map.52 = (f32[32,32,128]{2,1,0:T(8,128)}, f32[32,32,128]{2,1,0:T(8,128)}) custom-call(f32[66,32,128]{2,1,0:T(8,128)S(1)} %collective-permute-done.2.seg0, f32[66,32,128]{2,1,0:T(8,128)S(1)} %get-tuple-element.12.seg1, f32[66,32,128]{2,1,0:T(8,128)S(1)} %get-tuple-element.11.seg2, f32[66,32,128]{2,1,0:T(8,128)} %collective-permute-done.3.seg3_any, ...), custom_call_target="tpu_custom_call" | custom-call | bytes 20971520 | tf_op jit(solution)/shard_map/pallas_call | solution.py:327
  (1 shorter events, 0.0 us)
Async XLA Ops:
  0.6 39.7 %copy-start.1 = (f32[32,32,128]{2,1,0:T(8,128)S(1)}, f32[32,32,128]{2,1,0:T(8,128)}, u32[]{:S(2)}) copy-start(f32[32,32,128]{2,1,0:T(8,128)} %potential.1) | copy-start | bytes 1572868
  0.6 39.7 %copy-start = (f32[32,32,128]{2,1,0:T(8,128)S(1)}, f32[32,32,128]{2,1,0:T(8,128)}, u32[]{:S(2)}) copy-start(f32[32,32,128]{2,1,0:T(8,128)} %source.1) | copy-start | bytes 1572868
  3.1 37.3 %collective-permute-start = (f32[129,8,128]{2,1,0:T(8,128)}, f32[129,8,128]{2,1,0:T(8,128)S(1)}, u32[]{:S(2)}, u32[]{:S(2)}) collective-permute-start(f32[129,8,128]{2,1,0:T(8,128)} %get-tuple-element.8), channel_id=1, source_target_pairs={{0,1},{1,2},{2,3},{3,4},{4,5},{5,6},{6,7},{7,8},{8,9},{9,10},{10,1... | collective-permute-start | bytes 1585160 | tf_op jit(solution)/shard_map/ppermute | solution.py:316
  7.0 33.3 %collective-permute-start.1 = (f32[129,8,128]{2,1,0:T(8,128)}, f32[129,8,128]{2,1,0:T(8,128)S(1)}, u32[]{:S(2)}, u32[]{:S(2)}) collective-permute-start(f32[129,8,128]{2,1,0:T(8,128)} %get-tuple-element.9), channel_id=1, source_target_pairs={{1,0},{2,1},{3,2},{4,3},{5,4},{6,5},{7,6},{8,7},{9,8},{10,9},{11,1... | collective-permute-start | bytes 1585160 | tf_op jit(solution)/shard_map/ppermute | solution.py:316
  41.1 25.3 %collective-permute-start.2 = (f32[66,32,128]{2,1,0:T(8,128)S(1)}, f32[66,32,128]{2,1,0:T(8,128)S(1)}, u32[]{:S(2)}, u32[]{:S(2)}) collective-permute-start(f32[66,32,128]{2,1,0:T(8,128)S(1)} %get-tuple-element.11.seg2), channel_id=1, source_target_pairs={{0,32},{32,64},{64,96},{96,128},{128,160},{160,192},{192,224},{224... | collective-permute-start | bytes 3244040 | tf_op jit(solution)/shard_map/ppermute | solution.py:316
  44.3 22.1 %collective-permute-start.3 = (f32[66,32,128]{2,1,0:T(8,128)S(1)}, f32[66,32,128]{2,1,0:T(8,128)}, u32[]{:S(2)}, u32[]{:S(2)}) collective-permute-start(f32[66,32,128]{2,1,0:T(8,128)S(1)} %get-tuple-element.12.seg1), channel_id=1, source_target_pairs={{32,0},{64,32},{96,64},{128,96},{160,128},{192,160},{224,192},{256... | collective-permute-start | bytes 3244040 | tf_op jit(solution)/shard_map/ppermute | solution.py:316
  46.3 20.2 %all-to-all-start.1 = ((f32[32,1,128]{2,1,0:T(1,128)}), f32[32,1,128]{2,1,0:T(1,128)S(1)}, u32[]{:S(2)}, u32[]{:S(2)}) async-start(f32[32,1,128]{2,1,0:T(1,128)} %bitcast.3), calls=%async_computation.1 | async-start | bytes 32768 | tf_op jit(solution)/shard_map/all_to_all | solution.py:323

commit v4 on v3

--- a/solution.py
+++ b/solution.py
@@ -88,7 +88,19 @@
     part[...] = jnp.where(rows_of(part.shape[0]) % 2 == 0, total, flags[:1])
 
 
-def middle_kernel(source, potential, low, high, parts, first_half, second_half, part):
+def middle_kernel(source, potential, low, high, parts, across, beyond, part):
+    even = lax.axis_index(GROUP) % 2 == 0
+
+    @pl.when(even)
+    def _():
+        middle(source, potential, low, high, parts, beyond, across, part)
+
+    @pl.when(jnp.logical_not(even))
+    def _():
+        middle(source, potential, low, high, parts, across, beyond, part)
+
+
+def middle(source, potential, low, high, parts, first_half, second_half, part):
     row = rows_of(parts.shape[0])
     mine = jnp.where(row == 2 * lax.axis_index(GROUP) + 1, parts[...], 0.0)
     own = jnp.broadcast_to(jnp.sum(mine, axis=0, keepdims=True), (KH, NZ))
@@ -121,11 +133,19 @@
     return left + right
 
 
-def cycle_kernel(
-    cells, seg0, seg1, seg2, seg3_any, parts, place, smoothed, residual, red, black, coarse, corr, seg3, sem
-):
-    load = pltpu.make_async_copy(seg3_any, seg3, sem)
-    load.start()
+def cycle_kernel(cells, from_across, across, beyond, from_beyond, parts, place, *refs):
+    even = place[0] % 2 == 0
+
+    @pl.when(even)
+    def _():
+        cycle(cells, from_beyond, beyond, across, from_across, parts, place, *refs)
+
+    @pl.when(jnp.logical_not(even))
+    def _():
+        cycle(cells, from_across, across, beyond, from_beyond, parts, place, *refs)
+
+
+def cycle(cells, seg0, seg1, seg2, seg3, parts, place, smoothed, residual, red, black, coarse, corr):
     segments = (seg0, seg1, seg2, seg3)
     total = jnp.sum(jnp.sum(parts[...], axis=0, keepdims=True), axis=1, keepdims=True)
     mean = total * (1.0 / cells)
@@ -151,8 +171,6 @@
     row = rows_of(NK)
     whole = slice(PAD, PAD + NK)
     for x in range(NX):
-        if x + 1 == 3 * H:
-            load.wait()
         centre = field(1, x)
         before = field(1, x - 1) if x > 0 else seg0[EXTRA]
         after = field(1, x + 1) if x < NX - 1 else seg3[EXTRA]
@@ -292,7 +310,7 @@
     padded = pltpu.VMEM((NX, NK + 2 * PAD, NZ), F32)
     return call(
         functools.partial(cycle_kernel, cells),
-        [VMEM, VMEM, VMEM, ANY, VMEM, SMEM],
+        [VMEM] * 5 + [SMEM],
         [shape(N, N, NZ), shape(N, N, NZ)],
         9,
         20,
@@ -301,8 +319,6 @@
             padded,
             pltpu.VMEM((NC, NK, NZ), F32),
             pltpu.VMEM((NC, NK + 2 * PAD, NZ), F32),
-            pltpu.VMEM((SEGMENT, NK, NZ), F32),
-            pltpu.SemaphoreType.DMA,
         ],
     )
 
@@ -318,13 +334,15 @@
     up, down, part = build_pack(groups)(source, potential, refined)
     low, high = both_ways(up, down, MEMBER)
     parts = lax.all_to_all(part, GROUP, 0, 0, tiled=True)
-    first_half, second_half, part = build_middle(members)(source, potential, low, high, parts)
-    before, after = both_ways(second_half, first_half, GROUP)
+    across, beyond, part = build_middle(members)(source, potential, low, high, parts)
+    swaps = [[p for i in range(c, groups - 1, 2) for p in ((i, i + 1), (i + 1, i))] for c in range(2)]
+    from_across = lax.ppermute(across, GROUP, swaps[0])
+    from_beyond = lax.ppermute(beyond, GROUP, swaps[1])
     parts = lax.all_to_all(part, MEMBER, 0, 0, tiled=True)
     place = jnp.stack(
         [lax.axis_index(GROUP), lax.axis_index(MEMBER), jnp.int32(groups), jnp.int32(members)]
     ).astype(jnp.int32)
-    return build_cycle(groups * members * N * N * NZ)(before, first_half, second_half, after, parts, place)
+    return build_cycle(groups * members * N * N * NZ)(from_across, across, beyond, from_beyond, parts, place)
 
 
 def solution(mesh):

time: 73.6 us -> 74 us (level)
    ppermute x0 -> x2, starting transfers between devices: none -> 5.11 us  [the longest x1 3.02 us: per_device(): from_across = lax.ppermute(across, GROUP, swaps[0])]
    ppermute x2 -> x1, starting transfers between devices: 7.17 us -> 3.98 us  [both_ways(): lax.ppermute(up, axis, pairs)]
    ppermute x2 -> x1, starting transfers between devices: 3.21 us -> 1.29 us  [both_ways(): lax.ppermute(down, axis, [(b, a) for a, b in pairs])]
where the time goes in v4:
time: 74 us; the launch traced here: 73.7 us
  blocking collectives  32 us (43%)
  starting transfers between devices  22 us (30%)
  Pallas kernels  10.4 us (14%)
  waiting for transfers between devices  8.43 us (11%)
    all_to_all x1, blocking collectives, per_device(): parts = lax.all_to_all(part, GROUP, 0, 0, tiled=True)  32 us
    all_to_all x1, starting transfers between devices, per_device(): parts = lax.all_to_all(part, MEMBER, 0, 0, tiled=True)  11.7 us
    all_to_all x1, waiting for transfers between devices, per_device(): parts = lax.all_to_all(part, MEMBER, 0, 0, tiled=True)  8.42 us
    pallas_call x1, Pallas kernels, per_device(): build_cycle(groups * members * N * N * NZ)  7.21 us
    ppermute x1, starting transfers between devices, both_ways(): lax.ppermute(up, axis, pairs)  3.98 us
    ppermute x1, starting transfers between devices, per_device(): from_across = lax.ppermute(across, GROUP, swaps[0])  3.02 us
    pallas_call x1, Pallas kernels, per_device(): up, down, part = build_pack(groups)(source, potential, refined)  2.39 us
    ppermute x1, starting transfers between devices, per_device(): from_beyond = lax.ppermute(beyond, GROUP, swaps[1])  2.09 us
  transfers between devices with their start and end apart: 5, of which 1 were waited for; matrix products, arithmetic and copies ran while one was open for 0% of the time, Pallas kernels for 0%

profile of v4, /device:TPU:1, one launch (start us, length us, event | category | flops | bytes accessed | tf_op | source)
XLA Modules:
  0.0 73.7 jit_solution(11699432221723636507)
XLA Ops:
  0.6 0.0 copy-start.1
  0.6 0.0 copy-start
  0.6 2.4 %shard_map.50 = (f32[129,8,128]{2,1,0:T(8,128)}, f32[129,8,128]{2,1,0:T(8,128)}, f32[64,128]{1,0:T(8,128)}) custom-call(f32[32,32,128]{2,1,0:T(8,128)} %source.1, f32[32,32,128]{2,1,0:T(8,128)} %potential.1, s32[1,1,4]{2,1,0:T(1,128)} %refined_any.1), custom_call_target="tpu_custom_call" | custom-call | bytes 4194304 | tf_op jit(solution)/shard_map/pallas_call | solution.py:334
  3.1 4.0 %collective-permute-start = (f32[129,8,128]{2,1,0:T(8,128)}, f32[129,8,128]{2,1,0:T(8,128)S(1)}, u32[]{:S(2)}, u32[]{:S(2)}) collective-permute-start(f32[129,8,128]{2,1,0:T(8,128)} %get-tuple-element.8), channel_id=1, source_target_pairs={{0,1},{1,2},{2,3},{3,4},{4,5},{5,6},{6,7},{7,8},{8,9},{9,10},{10,1... | collective-permute-start | bytes 1585160 | tf_op jit(solution)/shard_map/ppermute | solution.py:332
  7.0 1.3 %collective-permute-start.1 = (f32[129,8,128]{2,1,0:T(8,128)}, f32[129,8,128]{2,1,0:T(8,128)S(1)}, u32[]{:S(2)}, u32[]{:S(2)}) collective-permute-start(f32[129,8,128]{2,1,0:T(8,128)} %get-tuple-element.9), channel_id=1, source_target_pairs={{1,0},{2,1},{3,2},{4,3},{5,4},{6,5},{7,6},{8,7},{9,8},{10,9},{11,1... | collective-permute-start | bytes 1585160 | tf_op jit(solution)/shard_map/ppermute | solution.py:332
  8.3 32.0 %all_to_all.22 = f32[32,2,128]{2,1,0:T(2,128)S(1)} all-to-all(f32[32,2,128]{2,1,0:T(2,128)} %bitcast.10), channel_id=1, replica_groups=mesh['group'=32,'member'=32] {'group'}, dimensions={0} | all-to-all | bytes 65536 | tf_op jit(solution)/shard_map/all_to_all | solution.py:336
  40.3 0.0 collective-permute-done.low
  40.3 0.0 collective-permute-done.1.high
  40.3 0.0 copy-done.1
  40.3 0.0 copy-done
  40.4 0.8 %shard_map.51 = (f32[66,32,128]{2,1,0:T(8,128)S(1)}, f32[66,32,128]{2,1,0:T(8,128)S(1)}, f32[32,128]{1,0:T(8,128)}) custom-call(f32[32,32,128]{2,1,0:T(8,128)S(1)} %copy-done, f32[32,32,128]{2,1,0:T(8,128)S(1)} %copy-done.1, f32[129,8,128]{2,1,0:T(8,128)S(1)} %collective-permute-done.low, f32[129,8,128]{2,1,0:T(8,128)S(1)} %collective-permute-done.1.high, ...), custom_call_target="tpu_custom_call" | custom-call | bytes 6291456 | tf_op jit(solution)/shard_map/pallas_call | solution.py:337
  41.1 3.0 %collective-permute-start.2 = (f32[66,32,128]{2,1,0:T(8,128)S(1)}, f32[66,32,128]{2,1,0:T(8,128)S(1)}, u32[]{:S(2)}, u32[]{:S(2)}) collective-permute-start(f32[66,32,128]{2,1,0:T(8,128)S(1)} %get-tuple-element.11.across), channel_id=1, source_target_pairs={{0,32},{32,0},{64,96},{96,64},{128,160},{160,128},{192,224},{224,1... | collective-permute-start | bytes 3244040 | tf_op jit(solution)/shard_map/ppermute | solution.py:339
  44.2 2.1 %collective-permute-start.3 = (f32[66,32,128]{2,1,0:T(8,128)S(1)}, f32[66,32,128]{2,1,0:T(8,128)}, u32[]{:S(2)}, u32[]{:S(2)}) collective-permute-start(f32[66,32,128]{2,1,0:T(8,128)S(1)} %get-tuple-element.12.beyond), channel_id=1, source_target_pairs={{32,64},{64,32},{96,128},{128,96},{160,192},{192,160},{224,256},{2... | collective-permute-start | bytes 3244040 | tf_op jit(solution)/shard_map/ppermute | solution.py:340
  46.3 11.7 %all-to-all-start.1 = ((f32[32,1,128]{2,1,0:T(1,128)}), f32[32,1,128]{2,1,0:T(1,128)S(1)}, u32[]{:S(2)}, u32[]{:S(2)}) async-start(f32[32,1,128]{2,1,0:T(1,128)} %bitcast.3), calls=%async_computation.1 | async-start | bytes 32768 | tf_op jit(solution)/shard_map/all_to_all | solution.py:341
  58.0 0.1 pad_add_fusion.place
  58.0 8.4 %all-to-all-done.1 = f32[32,1,128]{2,1,0:T(1,128)S(1)} async-done(((f32[32,1,128]{2,1,0:T(1,128)}), f32[32,1,128]{2,1,0:T(1,128)S(1)}, u32[]{:S(2)}, u32[]{:S(2)}) %all-to-all-start.1) | async-done | bytes 16416 | tf_op jit(solution)/shard_map/all_to_all | solution.py:341
  66.5 0.0 collective-permute-done.2.from_across
  66.5 0.0 collective-permute-done.3.from_beyond
  66.5 7.2 %shard_map.52 = (f32[32,32,128]{2,1,0:T(8,128)}, f32[32,32,128]{2,1,0:T(8,128)}) custom-call(f32[66,32,128]{2,1,0:T(8,128)S(1)} %collective-permute-done.2.from_across, f32[66,32,128]{2,1,0:T(8,128)S(1)} %get-tuple-element.11.across, f32[66,32,128]{2,1,0:T(8,128)S(1)} %get-tuple-element.12.beyond, f32[66,32,128]{2,1,0:T(8,128)} %collective-permute-done.3.from_beyond, ...), custom_call_target="tpu_custom_call" | custom-call | bytes 20971520 | tf_op jit(solution)/shard_map/pallas_call | solution.py:345
  (1 shorter events, 0.0 us)
Async XLA Ops:
  0.6 39.7 %copy-start.1 = (f32[32,32,128]{2,1,0:T(8,128)S(1)}, f32[32,32,128]{2,1,0:T(8,128)}, u32[]{:S(2)}) copy-start(f32[32,32,128]{2,1,0:T(8,128)} %potential.1) | copy-start | bytes 1572868
  0.6 39.7 %copy-start = (f32[32,32,128]{2,1,0:T(8,128)S(1)}, f32[32,32,128]{2,1,0:T(8,128)}, u32[]{:S(2)}) copy-start(f32[32,32,128]{2,1,0:T(8,128)} %source.1) | copy-start | bytes 1572868
  3.1 37.3 %collective-permute-start = (f32[129,8,128]{2,1,0:T(8,128)}, f32[129,8,128]{2,1,0:T(8,128)S(1)}, u32[]{:S(2)}, u32[]{:S(2)}) collective-permute-start(f32[129,8,128]{2,1,0:T(8,128)} %get-tuple-element.8), channel_id=1, source_target_pairs={{0,1},{1,2},{2,3},{3,4},{4,5},{5,6},{6,7},{7,8},{8,9},{9,10},{10,1... | collective-permute-start | bytes 1585160 | tf_op jit(solution)/shard_map/ppermute | solution.py:332
  7.0 33.3 %collective-permute-start.1 = (f32[129,8,128]{2,1,0:T(8,128)}, f32[129,8,128]{2,1,0:T(8,128)S(1)}, u32[]{:S(2)}, u32[]{:S(2)}) collective-permute-start(f32[129,8,128]{2,1,0:T(8,128)} %get-tuple-element.9), channel_id=1, source_target_pairs={{1,0},{2,1},{3,2},{4,3},{5,4},{6,5},{7,6},{8,7},{9,8},{10,9},{11,1... | collective-permute-start | bytes 1585160 | tf_op jit(solution)/shard_map/ppermute | solution.py:332
  41.1 25.3 %collective-permute-start.2 = (f32[66,32,128]{2,1,0:T(8,128)S(1)}, f32[66,32,128]{2,1,0:T(8,128)S(1)}, u32[]{:S(2)}, u32[]{:S(2)}) collective-permute-start(f32[66,32,128]{2,1,0:T(8,128)S(1)} %get-tuple-element.11.across), channel_id=1, source_target_pairs={{0,32},{32,0},{64,96},{96,64},{128,160},{160,128},{192,224},{224,1... | collective-permute-start | bytes 3244040 | tf_op jit(solution)/shard_map/ppermute | solution.py:339
  44.2 22.3 %collective-permute-start.3 = (f32[66,32,128]{2,1,0:T(8,128)S(1)}, f32[66,32,128]{2,1,0:T(8,128)}, u32[]{:S(2)}, u32[]{:S(2)}) collective-permute-start(f32[66,32,128]{2,1,0:T(8,128)S(1)} %get-tuple-element.12.beyond), channel_id=1, source_target_pairs={{32,64},{64,32},{96,128},{128,96},{160,192},{192,160},{224,256},{2... | collective-permute-start | bytes 3244040 | tf_op jit(solution)/shard_map/ppermute | solution.py:340
  46.3 20.2 %all-to-all-start.1 = ((f32[32,1,128]{2,1,0:T(1,128)}), f32[32,1,128]{2,1,0:T(1,128)S(1)}, u32[]{:S(2)}, u32[]{:S(2)}) async-start(f32[32,1,128]{2,1,0:T(1,128)} %bitcast.3), calls=%async_computation.1 | async-start | bytes 32768 | tf_op jit(solution)/shard_map/all_to_all | solution.py:341
